TPU v7x, 512 devices: a whole 4x8x8 slice. The times are simulated.
512 devices in a mesh: ctx: 64 (over y_hi, z, x), head: 8 (over y_lo, core).
Axes of the slice: x: 4, y: 8 (y_hi: 2, y_lo: 4; y = y_hi * 4 + y_lo), z: 8, core: 2. Of those that a mesh axis runs over, the one named last changes fastest.
Arguments:
- queries: bfloat16 [8, 8192, 128], P('head', 'ctx'), may hold values from -32 to 32
- keys: bfloat16 [8192, 128], P('ctx'), may hold values from -6 to 6
- values: bfloat16 [8192, 128], P('ctx'), may hold values from -6 to 6
- grad_out: bfloat16 [8, 8192, 128], P('head', 'ctx'), may hold values from -6 to 6
- order: int32 [128], replicated, may hold values from 0 to 127, each once
- segment: int32 [8192], replicated, may hold values from 0 to 5, as said below
Outputs:
- grad_queries: bfloat16 [8, 8192, 128], P('head', 'ctx')
- grad_keys: bfloat16 [8192, 128], P('ctx')
- grad_values: bfloat16 [8192, 128], P('ctx')
Inputs may be any that keep to these rules, and one draw needn't show every extreme that they name: `order`: a permutation of the 128 block numbers. `segment`: nondecreasing along positions; every document starts at an even position; ids 0 and 5 both occur.
All inputs are finite; a program needn't handle non-finite values.
Results may differ from a plain program's by a relative error of at most 0.0055.
Values may be sent and summed in bfloat16 or wider, within the bound.
A program may use at most 64 MiB of HBM per device.

v0:
```python
import math

import jax
import jax.numpy as jnp
from jax import lax
from jax.sharding import PartitionSpec as P

DOCS = 6


NEGATIVE = -1e30


def block_of(total):
    return max((d for d in range(1, min(total, 512) + 1) if total % d == 0))


def blockwise(count, step, carry):
    size = block_of(count)
    if size == count:
        return step(carry, 0, size)
    return lax.fori_loop(
        0, count // size, lambda index, state: step(state, index * size, size), carry
    )


def locate_every(order, segment, span):
    position = (order[:, None] * span + jnp.arange(span, dtype=jnp.int32)[None, :]).reshape(-1)
    bounds = jnp.arange(1, DOCS, dtype=jnp.int32)
    starts = jnp.sum((segment[None, :] < bounds[:, None]).astype(jnp.int32), axis=1)
    doc_ids = jnp.sum((position[:, None] >= starts[None, :]).astype(jnp.int32), axis=1)
    return (position, doc_ids)


def permitted(query_pos, query_doc, key_pos, key_doc):
    return (key_pos[None, :] <= query_pos[:, None]) & (key_doc[None, :] == query_doc[:, None])


def local(queries, keys, values, grad_out, order, segment):
    heads, rows, width = queries.shape
    span = rows // 2
    scale = 1.0 / math.sqrt(width)
    every_pos, every_doc = locate_every(order, segment, span)

    def locate(first, size):
        return (
            lax.dynamic_slice_in_dim(every_pos, first, size, 0),
            lax.dynamic_slice_in_dim(every_doc, first, size, 0),
        )

    my_pos, my_doc = locate(lax.axis_index("ctx") * rows, rows)

    def key_block(pieces, start, offset, size):
        block_keys = lax.dynamic_slice_in_dim(pieces[0], offset, size, 0)
        block_values = lax.dynamic_slice_in_dim(pieces[1], offset, size, 0)
        key_pos, key_doc = locate(start + offset, size)
        allowed = permitted(my_pos, my_doc, key_pos, key_doc)[None]
        scores = (
            jnp.einsum("hqd,kd->hqk", queries, block_keys, preferred_element_type=jnp.float32)
            * scale
        )
        dprobs = jnp.einsum(
            "hqd,kd->hqk", grad_out, block_values, preferred_element_type=jnp.float32
        )
        return (block_keys, allowed, scores, dprobs)

    start_state = (
        jnp.full((heads, rows), NEGATIVE, jnp.float32),
        jnp.zeros((heads, rows), jnp.float32),
        jnp.zeros((heads, rows), jnp.float32),
    )
    grad_start = jnp.zeros((heads, rows, width), jnp.float32)
    stats = {}
    pieces = (
        lax.all_gather(keys, "ctx", axis=0, tiled=True),
        lax.all_gather(values, "ctx", axis=0, tiled=True),
    )
    start = jnp.int32(0)

    def step(inner, offset, size):
        peak, total, weighted = inner
        block_keys, allowed, scores, dprobs = key_block(pieces, start, offset, size)
        new_peak = jnp.maximum(peak, jnp.max(jnp.where(allowed, scores, NEGATIVE), axis=2))
        expo = jnp.where(allowed, jnp.exp(scores - new_peak[:, :, None]), 0.0)
        factor = jnp.exp(peak - new_peak)
        return (
            new_peak,
            total * factor + jnp.sum(expo, axis=2),
            weighted * factor + jnp.sum(expo * dprobs, axis=2),
        )

    peak, total, weighted = blockwise(pieces[0].shape[0], step, start_state)
    stats["lse"] = peak + jnp.log(total)
    stats["delta"] = weighted / total
    query_pieces = (
        lax.all_gather(keys, "ctx", axis=0, tiled=True),
        lax.all_gather(values, "ctx", axis=0, tiled=True),
    )
    query_start = jnp.int32(0)

    def step(inner, offset, size):
        block_keys, allowed, scores, dprobs = key_block(query_pieces, query_start, offset, size)
        probs = jnp.where(allowed, jnp.exp(scores - stats["lse"][:, :, None]), 0.0)
        dscores = (probs * (dprobs - stats["delta"][:, :, None]) * scale).astype(jnp.bfloat16)
        return inner + jnp.einsum(
            "hqk,kd->hqd", dscores, block_keys, preferred_element_type=jnp.float32
        )

    grad_q = blockwise(query_pieces[0].shape[0], step, grad_start)
    all_lse, all_delta = (
        lax.all_gather(stats["lse"], "ctx", axis=1, tiled=True),
        lax.all_gather(stats["delta"], "ctx", axis=1, tiled=True),
    )
    empty = jnp.zeros((rows, width), jnp.float32)
    key_start = jnp.int32(0)
    piece_q = lax.all_gather(queries, "ctx", axis=1, tiled=True)
    piece_go = lax.all_gather(grad_out, "ctx", axis=1, tiled=True)

    def step(inner, offset, size):
        grad_k, grad_v = inner
        block_q = lax.dynamic_slice_in_dim(piece_q, offset, size, 1)
        block_go = lax.dynamic_slice_in_dim(piece_go, offset, size, 1)
        block_lse = lax.dynamic_slice_in_dim(all_lse, key_start + offset, size, 1)
        block_delta = lax.dynamic_slice_in_dim(all_delta, key_start + offset, size, 1)
        query_pos, query_doc = locate(key_start + offset, size)
        allowed = permitted(query_pos, query_doc, my_pos, my_doc)[None]
        scores = (
            jnp.einsum("hqd,kd->hqk", block_q, keys, preferred_element_type=jnp.float32) * scale
        )
        probs = jnp.where(allowed, jnp.exp(scores - block_lse[:, :, None]), 0.0)
        dprobs = jnp.einsum("hqd,kd->hqk", block_go, values, preferred_element_type=jnp.float32)
        dscores = (probs * (dprobs - block_delta[:, :, None]) * scale).astype(jnp.bfloat16)
        grad_k = grad_k + jnp.einsum(
            "hqk,hqd->kd", dscores, block_q, preferred_element_type=jnp.float32
        )
        grad_v = grad_v + jnp.einsum(
            "hqk,hqd->kd", probs.astype(jnp.bfloat16), block_go, preferred_element_type=jnp.float32
        )
        return (grad_k, grad_v)

    grad_k, grad_v = blockwise(piece_q.shape[1], step, (empty, empty))
    grad_k, grad_v = lax.psum((grad_k, grad_v), "head")
    return (grad_q.astype(jnp.bfloat16), grad_k.astype(jnp.bfloat16), grad_v.astype(jnp.bfloat16))


def solution(mesh):
    placed = (
        P("head", "ctx", None),
        P("ctx", None),
        P("ctx", None),
        P("head", "ctx", None),
        P(),
        P(),
    )
    return jax.shard_map(
        local,
        mesh=mesh,
        in_specs=placed,
        out_specs=(P("head", "ctx", None), P("ctx", None), P("ctx", None)),
        check_vma=False,
    )
```

profile of v0, /device:TPU:1, one launch (start us, length us, event | category | flops | bytes accessed | tf_op | source)
XLA Modules:
  0.0 898.6 jit_solution(859204078719044062)
XLA Ops:
  12.2 135.2 %all-gather.5.cloned.1.call-done = bf16[8192,128]{1,0:T(8,128)(2,1)} async-done(((bf16[128,128]{1,0:T(8,128)(2,1)}), bf16[8192,128]{1,0:T(8,128)(2,1)}) %all-gather.5.cloned.1.call-update) | async-done | bytes 2097168 | tf_op jit(solution)/shard_map/all_gather | solution.py:96
  147.4 133.9 %all-gather.7.cloned.1.call-done = bf16[8192,128]{1,0:T(8,128)(2,1)} async-done(((bf16[128,128]{1,0:T(8,128)(2,1)}), bf16[8192,128]{1,0:T(8,128)(2,1)}) %all-gather.7.cloned.1.call-update) | async-done | bytes 2097168 | tf_op jit(solution)/shard_map/all_gather | solution.py:97
  281.3 43.8 %while.48 = (s32[]{:T(128)}, f32[1,128]{1,0:T(1,128)S(1)}, f32[1,128]{1,0:T(1,128)S(1)}, f32[1,128]{1,0:T(1,128)S(1)}, s32[8192]{0:T(1024)S(1)}, /*index=5*/s32[...) while((s32[]{:T(128)}, f32[1,128]{1,0:T(1,128)S(1)}, ...), condition=%wide.region_6.7_spmd.clone, body=%wide.region_2.6_spmd.clone.sunk | while | flops 34800516 | bytes 1147110 | solution.py:22
  325.1 43.9 %while.49 = (s32[]{:T(128)}, f32[1,128,128]{2,1,0:T(8,128)S(1)}, s32[8192]{0:T(1024)S(1)}, s32[128]{0:T(128)S(1)}, s32[8192]{0:T(1024)S(1)}, /*index=5*/s32[128]...) while((s32[]{:T(128)}, f32[1,128,128]{2,1,0:T(8,128)S(1)}, ...), condition=%wide.region_8.9_spmd.clone, body=%wide.region_7.8_spmd.clone.sunk | while | flops 51019780 | bytes 1130208 | solution.py:22
  326.5 1.4 fusion.99
  329.2 1.4 fusion.99
  331.9 1.4 fusion.99
  334.7 1.4 fusion.99
  337.4 1.4 fusion.99
  340.2 1.4 fusion.99
  342.9 1.4 fusion.99
  345.7 1.4 fusion.99
  348.4 1.4 fusion.99
  351.1 1.4 fusion.99
  353.9 1.4 fusion.99
  356.6 1.4 fusion.99
  359.4 1.4 fusion.99
  362.1 1.4 fusion.99
  364.9 1.4 fusion.99
  367.6 1.4 fusion.99
  369.7 188.6 %all_gather.23 = f32[1,8192]{1,0:T(1,128)S(1)} all-gather(f32[1,128]{1,0:T(1,128)S(1)} %get-tuple-element.1241), channel_id=1, replica_groups=mesh['ctx'=64,'head'=8] {'ctx'}, dimensions={1}, use_global_device_ids=true | all-gather | bytes 33280 | tf_op jit(solution)/shard_map/all_gather | solution.py:111
  558.3 183.7 %all_gather.25 = f32[1,8192]{1,0:T(1,128)S(1)} all-gather(f32[1,128]{1,0:T(1,128)S(1)} %get-tuple-element.1236), channel_id=1, replica_groups=mesh['ctx'=64,'head'=8] {'ctx'}, dimensions={1}, use_global_device_ids=true | all-gather | bytes 33280 | tf_op jit(solution)/shard_map/all_gather | solution.py:112
  742.0 63.3 %while.50 = (s32[]{:T(128)}, f32[128,128]{1,0:T(8,128)S(1)}, f32[128,128]{1,0:T(8,128)S(1)}, s32[128]{0:T(128)S(1)}, s32[8192]{0:T(1024)S(1)}, /*index=5*/s32[12...) while((s32[]{:T(128)}, f32[128,128]{1,0:T(8,128)S(1)}, ...), condition=%wide.region_10.11_spmd.clone, body=%wide.region_9.10_spmd.clone.sunk | while | flops 67895296 | bytes 1665777 | solution.py:22
  805.4 86.7 %all-reduce.2 = (bf16[128,128]{1,0:T(8,128)(2,1)}, bf16[128,128]{1,0:T(8,128)(2,1)}) all-reduce(f32[128,128]{1,0:T(8,128)S(1)} %get-tuple-element.622, f32[128,128]{1,0:T(8,128)S(1)} %get-tuple-element.623), channel_id=1, replica_groups=mesh['ctx'=64,'head'=8] {'head'}, use_global_device_ids=true, to_apply=%region_11.12 | all-reduce | flops 32768 | bytes 196608 | tf_op jit(solution)/shard_map/psum | solution.py:142
  (302 shorter events, 131.7 us)
Async XLA Ops:
  7.2 140.3 %all-gather.5.cloned.1.call-start = ((), (), s32[]{:S(2)}) async-start(), calls=%async_computation | async-start | bytes 2129920 | tf_op jit(solution)/shard_map/all_gather | solution.py:96
  7.9 273.4 %all-gather.7.cloned.1.call-start = ((), (), s32[]{:S(2)}) async-start(), calls=%async_computation.1 | async-start | bytes 2129920 | tf_op jit(solution)/shard_map/all_gather | solution.py:97
  8.6 733.4 %all-gather.9.cloned.1.call-start = ((), (), s32[]{:S(2)}) async-start(), calls=%async_computation.2 | async-start | bytes 2129920 | tf_op jit(solution)/shard_map/all_gather | solution.py:116
  9.4 732.7 %all-gather.11.cloned.1.call-start = ((), (), s32[]{:S(2)}) async-start(), calls=%async_computation.3 | async-start | bytes 2129920 | tf_op jit(solution)/shard_map/all_gather | solution.py:117
  325.1 416.9 %copy-start = (bf16[128,128]{1,0:T(8,128)(2,1)S(1)}, bf16[128,128]{1,0:T(8,128)(2,1)}, u32[]{:S(2)}) copy-start(bf16[128,128]{1,0:T(8,128)(2,1)} %param.14) | copy-start | bytes 98308
  325.1 416.9 %copy-start.1 = (bf16[128,128]{1,0:T(8,128)(2,1)S(1)}, bf16[128,128]{1,0:T(8,128)(2,1)}, u32[]{:S(2)}) copy-start(bf16[128,128]{1,0:T(8,128)(2,1)} %param.13) | copy-start | bytes 98308
Sparse Core Ops, SparseCore 0:
  12.4 135.0 all-gather.4
  151.8 129.5 all-gather.6
  285.7 129.9 all-gather.8
  419.9 129.5 all-gather.10
where the time goes:
time: 904 us; the launch traced here: 899 us
  blocking collectives  459 us (51%)
  waiting for transfers between devices  272 us (30%)
  matrix products  137 us (15%)
  between operations  13.9 us (2%)
    all_gather x1, blocking collectives, local(): lax.all_gather(stats['lse'], 'ctx', axis=1, tiled=True)  189 us
    all_gather x1, blocking collectives, local(): lax.all_gather(stats['delta'], 'ctx', axis=1, tiled=True)  184 us
    all_gather x1, waiting for transfers between devices, local(): lax.all_gather(keys, 'ctx', axis=0, tiled=True)  135 us
    all_gather x1, waiting for transfers between devices, local(): lax.all_gather(values, 'ctx', axis=0, tiled=True)  134 us
    psum x1, blocking collectives, local(): grad_k, grad_v = lax.psum((grad_k, grad_v), 'head')  86.7 us
    dot_general x32, matrix products, key_block(): jnp.einsum('hqd,kd->hqk', queries, block_keys, preferred_element_type=jnp...  36.5 us
    dot_general x16, matrix products, step(): jnp.einsum('hqk,kd->hqd', dscores, block_keys, preferred_element_type=jnp...  22.6 us
    dot_general x16, matrix products, step(): jnp.einsum('hqk,hqd->kd', dscores, block_q, preferred_element_type=jnp.fl...  22.3 us
  transfers between devices with their start and end apart: 4, of which 2 were waited for; matrix products, arithmetic and copies ran while one was open for 10% of the time, Pallas kernels for 0%

commit v1 on v0

v1 whole, which is shorter than its diff:
```python
import functools
import math

import jax
import jax.numpy as jnp
from jax import lax
from jax.experimental import pallas as pl
from jax.experimental.pallas import tpu as pltpu
from jax.sharding import PartitionSpec as P

YH, Z, X, YL, CORES = 2, 8, 4, 4, 2
DOCS = 6
SPAN = 64
ROWS = 2 * SPAN
WIDTH = 128
TILE = 1024
LANES = 256
PARTS = TILE // LANES
CHUNK = 128
NEGATIVE = -1e30
FLOOR = -1e20
MESH = pl.DeviceIdType.MESH
SCALE = 1.0 / math.sqrt(WIDTH)
LOG2E = 1.4426950408889634
NT = (((1,), (1,)), ((), ()))
TN = (((0,), (0,)), ((), ()))


def device(yh, z, x, yl, c):
    return {"ctx": yh * (Z * X) + z * X + x, "head": yl * CORES + c}


def kernel(
    order, segment, q_in, k_in, v_in, go_in, dq_out, dk_out, dv_out,
    qbuf, kv, kbuf, scores, dprobs, pair, peaks, lows, highs, stats,
    give, take, total, gathered, pieces, dq_part, dq_took,
    local_sem, send_sem, recv_sem, swap_sem,
):
    i, h = lax.axis_index("ctx"), lax.axis_index("head")
    yh, z, x = lax.div(i, Z * X), lax.rem(lax.div(i, X), Z), lax.rem(i, X)
    yl, c = lax.div(h, CORES), lax.rem(h, CORES)
    yp, yj = lax.rem(yl, 2), lax.div(yl, 2)
    own = yp * X + x
    sibling = device(yh, z, x, yl, 1 - c)

    def query_peer(n):
        tx = lax.rem(x + lax.rem(n, X), X)
        tp = lax.rem(yp + lax.div(n, X), 2)
        return device(yh, z, tx, yj * 2 + tp, c), tp * X + tx

    def near_peer(n):
        return device(yh, lax.rem(z + n, Z), x, yl, c)

    def far_peer(n):
        return device(1 - yh, lax.rem(z + n, Z), x, YL - 1 - yl, c)

    def owner(n):
        g, dz, jj = lax.div(n, 16), lax.rem(lax.div(n, 2), Z), lax.rem(n, 2)
        tj = lax.rem(yj + jj, 2)
        where = device(lax.rem(yh + g, 2), lax.rem(z + Z - dz, Z), x, tj * 2 + yp, c)
        return where, lax.div(n, 2) * SPAN + tj * 32

    def head_peer(n):
        return device(yh, z, x, lax.rem(yl + lax.div(n, 2), YL), lax.rem(c + n, 2))

    def remote(src, dst, send, recv, where):
        return pltpu.make_async_remote_copy(
            src_ref=src, dst_ref=dst, send_sem=send, recv_sem=recv,
            device_id=where, device_id_type=MESH,
        )

    def wait_for(ref, sem):
        pltpu.make_async_copy(ref, ref, sem).wait()

    def loop(first, last, body):
        def step(n, carry):
            body(n)
            return carry

        lax.fori_loop(first, last, step, 0)

    mine = pl.ds(pl.multiple_of(own * ROWS, ROWS), ROWS)
    loads = [
        pltpu.make_async_copy(k_in, kv.at[0], local_sem.at[0]),
        pltpu.make_async_copy(v_in, kv.at[1], local_sem.at[1]),
        pltpu.make_async_copy(q_in.at[0], qbuf.at[0, mine], local_sem.at[2]),
        pltpu.make_async_copy(go_in.at[0], qbuf.at[1, mine], local_sem.at[3]),
    ]
    for copy in loads:
        copy.start()

    barrier = pltpu.get_barrier_semaphore()

    def greet(where):
        pl.semaphore_signal(barrier, inc=1, device_id=where, device_id_type=MESH)

    loop(1, 32, lambda n: greet(owner(n)[0]))
    loop(0, 8, lambda n: greet(far_peer(n)))
    loop(1, 8, lambda n: greet(query_peer(n)[0]))
    loop(1, 8, lambda n: greet(head_peer(n)))

    for copy in loads:
        copy.wait()
    half = pl.ds(pl.multiple_of(yp * SPAN, SPAN), SPAN)
    other = pl.ds(pl.multiple_of((1 - yp) * SPAN, SPAN), SPAN)
    kbuf[:, :SPAN] = kv[:, half]

    pl.semaphore_wait(barrier, 31 + 8 + 7 + 7)

    def send_far(n):
        rows = pl.ds(pl.multiple_of(512 + n * SPAN, SPAN), SPAN)
        remote(kv.at[c, other], kbuf.at[c, rows], send_sem.at[0], recv_sem.at[1], far_peer(n)).start()

    def send_near(n):
        rows = pl.ds(pl.multiple_of(n * SPAN, SPAN), SPAN)
        remote(kv.at[c, half], kbuf.at[c, rows], send_sem.at[0], recv_sem.at[0], near_peer(n)).start()

    def send_query(n):
        remote(qbuf.at[:, mine], qbuf.at[:, mine], send_sem.at[1], recv_sem.at[2], query_peer(n)[0]).start()

    loop(0, 8, send_far)
    loop(1, 8, send_near)
    loop(1, 8, send_query)

    docs = segment[...]
    starts = [
        jnp.sum((docs < d).astype(jnp.int32), axis=(0, 1), keepdims=True) for d in range(1, DOCS)
    ]
    lane = lax.broadcasted_iota(jnp.int32, (8, ROWS), 1)
    for s in range(X):
        ctx = yh * (Z * X) + z * X + s
        first, second = order[2 * ctx], order[2 * ctx + 1]
        place = jnp.where(lane < SPAN, first * SPAN + lane, second * SPAN + lane - SPAN)
        low = jnp.zeros_like(place)
        for start in starts:
            low = jnp.maximum(low, jnp.where(start <= place, start, 0))
        for t in (s, s + X):
            lows[t // 2, :, (t % 2) * ROWS : (t % 2 + 1) * ROWS] = low
            highs[t // 2, :, (t % 2) * ROWS : (t % 2 + 1) * ROWS] = place

    wait_for(kbuf.at[0, pl.ds(SPAN, 448)], recv_sem.at[0])
    near = kbuf.at[c, pl.ds(SPAN, 448)]
    swap_near = remote(near, near, swap_sem.at[0], swap_sem.at[1], sibling)
    swap_near.start()
    wait_for(kbuf.at[0, pl.ds(512, 512)], recv_sem.at[1])
    far = kbuf.at[c, pl.ds(512, 512)]
    swap_far = remote(far, far, swap_sem.at[2], swap_sem.at[3], sibling)
    swap_far.start()
    wait_for(qbuf.at[:, pl.ds(ROWS, 7 * ROWS)], recv_sem.at[2])

    row = lax.broadcasted_iota(jnp.int32, (SPAN, LANES), 0)

    def product(g, t):
        rows = pl.ds(pl.multiple_of(t * LANES, LANES), LANES)
        low, high = lows[t, 0:1, :], highs[t, 0:1, :]
        s = lax.dot_general(
            kbuf[0, g * 512 : g * 512 + 512], qbuf[0, rows], NT, preferred_element_type=jnp.float32
        )
        peak = None if g == 0 else peaks[t]
        for n in range(8):
            ctx = lax.rem(yh + g, 2) * (Z * X) + lax.rem(z + Z - n, Z) * X + x
            place = order[2 * ctx + yp] * SPAN + row
            masked = jnp.where(
                (place >= low) & (place <= high), s[n * SPAN : n * SPAN + SPAN], NEGATIVE
            )
            scores[t, g * 512 + n * SPAN : g * 512 + n * SPAN + SPAN] = masked
            top = jnp.max(masked.reshape(SPAN // 8, 8, LANES), axis=0)
            peak = top if peak is None else jnp.maximum(peak, top)
        peaks[t] = peak
        dprobs[t, g * 512 : g * 512 + 512] = lax.dot_general(
            kbuf[1, g * 512 : g * 512 + 512], qbuf[1, rows], NT, preferred_element_type=jnp.float32
        )

    swap_near.wait_recv()
    loop(0, PARTS, functools.partial(product, 0))
    swap_far.wait_recv()
    loop(0, PARTS, functools.partial(product, 1))

    def summed(a):
        return jnp.sum(a.reshape(CHUNK // 8, 8, LANES), axis=0)

    def weigh(t):
        peak = jnp.maximum(jnp.max(peaks[t], axis=0, keepdims=True), FLOOR)

        def step(r, carry):
            rows = pl.ds(pl.multiple_of(r * CHUNK, CHUNK), CHUNK)
            expo = jnp.exp2((scores[t, rows] - peak) * (SCALE * LOG2E))
            scores[t, rows] = expo
            return carry[0] + summed(expo), carry[1] + summed(expo * dprobs[t, rows])

        zero = jnp.zeros((8, LANES), jnp.float32)
        mass, weighted = lax.fori_loop(0, TILE // CHUNK, step, (zero, zero))
        mass = jnp.maximum(jnp.sum(mass, axis=0, keepdims=True), 1e-30)
        weighted = jnp.sum(weighted, axis=0, keepdims=True)
        peaks[t] = jnp.broadcast_to(peak * (SCALE * LOG2E), (8, LANES))
        stats[0, t, 0:1] = peak * (SCALE * LOG2E) + jnp.log2(mass)
        stats[0, t, 1:2] = weighted / mass

    loop(0, PARTS, weigh)

    def send_stats(n):
        remote(stats.at[0], stats.at[n], send_sem.at[2], recv_sem.at[3], query_peer(n)[0]).start()

    loop(1, 8, send_stats)
    wait_for(stats.at[pl.ds(1, 7)], recv_sem.at[3])

    def differentiate(t):
        every = [stats[n, t, 0:1] for n in range(8)]
        top = functools.reduce(jnp.maximum, every)
        shares = [jnp.exp2(e - top) for e in every]
        mass = functools.reduce(jnp.add, shares)
        delta = functools.reduce(jnp.add, [s * stats[n, t, 1:2] for n, s in enumerate(shares)]) / mass
        factor = jnp.exp2(peaks[t, 0:1] - top) / mass

        def step(r, carry):
            rows = pl.ds(pl.multiple_of(r * CHUNK, CHUNK), CHUNK)
            probs = scores[t, rows] * factor
            pair[1, t, rows] = probs.astype(jnp.bfloat16)
            pair[0, t, rows] = (probs * (dprobs[t, rows] - delta) * SCALE).astype(jnp.bfloat16)
            return carry

        lax.fori_loop(0, TILE // CHUNK, step, 0)

    loop(0, PARTS, differentiate)

    def key_side(which, r):
        rows = pl.ds(pl.multiple_of(r * LANES, LANES), LANES)
        acc = jnp.zeros((LANES, WIDTH), jnp.float32)
        for t in range(PARTS):
            acc += jnp.dot(
                pair[which, t, rows], qbuf[which, t * LANES : t * LANES + LANES],
                preferred_element_type=jnp.float32,
            )
        return acc, rows

    def give_away(r):
        acc, rows = key_side(1 - c, r)
        give[rows] = acc.astype(jnp.bfloat16)
        remote(give.at[rows], take.at[rows], send_sem.at[3], swap_sem.at[4 + r], sibling).start()

    loop(0, 4, give_away)

    def query_side(t):
        part = lax.dot_general(kbuf[0], pair[0, t], TN, preferred_element_type=jnp.float32)
        part = part.astype(dq_part.dtype)
        dq_part[2 * t] = part[:, :ROWS]
        dq_part[2 * t + 1] = part[:, ROWS:]

    loop(0, PARTS, query_side)

    def send_dq(n):
        where, slot = query_peer(n)
        remote(dq_part.at[slot], dq_took.at[n - 1], send_sem.at[4], recv_sem.at[4], where).start()

    loop(1, 8, send_dq)

    def send_piece(n):
        where, first = owner(n)
        rows = pl.ds(pl.multiple_of(first, 32), 32)
        remote(total.at[rows], gathered.at[n - 1], send_sem.at[5], recv_sem.at[5], where).start()

    def keep(r):
        acc, rows = key_side(c, r)
        wait_for(take.at[rows], swap_sem.at[4 + r])
        total[rows] = (acc + take[rows].astype(jnp.float32)).astype(jnp.bfloat16)
        loop(jnp.where(r == 0, 1, 8 * r), 8 * r + 8, send_piece)

    loop(0, 4, keep)

    wait_for(dq_took, recv_sem.at[4])
    dq = dq_part[own].astype(jnp.float32)
    for n in range(7):
        dq += dq_took[n].astype(jnp.float32)
    dq_out[0] = dq.T.astype(jnp.bfloat16)

    first = pl.ds(pl.multiple_of(yj * 32, 32), 32)
    wait_for(gathered, recv_sem.at[5])
    result = total[first].astype(jnp.float32)
    for n in range(31):
        result += gathered[n].astype(jnp.float32)
    pieces[0] = result.astype(jnp.bfloat16)

    def send_result(n):
        remote(pieces.at[0], pieces.at[n], send_sem.at[6], recv_sem.at[6], head_peer(n)).start()

    loop(1, 8, send_result)
    wait_for(pieces.at[pl.ds(1, 7)], recv_sem.at[6])
    for n in range(YL):
        fl = lax.rem(yl + YL - n, YL)
        rows = pl.ds(pl.multiple_of(lax.rem(fl, 2) * SPAN + lax.div(fl, 2) * 32, 32), 32)
        dk_out[rows] = pieces[2 * n + c]
        dv_out[rows] = pieces[2 * n + 1 - c]

    wait_for(kbuf.at[0, pl.ds(0, 960)], send_sem.at[0])
    wait_for(qbuf.at[:, pl.ds(ROWS, 7 * ROWS)], send_sem.at[1])
    swap_near.wait_send()
    swap_far.wait_send()
    wait_for(stats.at[pl.ds(1, 7)], send_sem.at[2])
    wait_for(give, send_sem.at[3])
    wait_for(dq_took, send_sem.at[4])
    wait_for(gathered, send_sem.at[5])
    wait_for(pieces.at[pl.ds(1, 7)], send_sem.at[6])


def local(queries, keys, values, grad_out, order, segment):
    bf16, f32, i32 = jnp.bfloat16, jnp.float32, jnp.int32
    smem, vmem, hbm = (
        pl.BlockSpec(memory_space=pltpu.SMEM),
        pl.BlockSpec(memory_space=pltpu.VMEM),
        pl.BlockSpec(memory_space=pl.ANY),
    )
    return pl.pallas_call(
        kernel,
        out_shape=(
            jax.ShapeDtypeStruct(queries.shape, bf16),
            jax.ShapeDtypeStruct(keys.shape, bf16),
            jax.ShapeDtypeStruct(values.shape, bf16),
        ),
        in_specs=[smem, vmem, hbm, hbm, hbm, hbm],
        out_specs=(vmem, vmem, vmem),
        scratch_shapes=[
            pltpu.VMEM((2, TILE, WIDTH), bf16),
            pltpu.VMEM((2, ROWS, WIDTH), bf16),
            pltpu.VMEM((2, TILE, WIDTH), bf16),
            pltpu.VMEM((PARTS, TILE, LANES), f32),
            pltpu.VMEM((PARTS, TILE, LANES), f32),
            pltpu.VMEM((2, PARTS, TILE, LANES), bf16),
            pltpu.VMEM((PARTS, 8, LANES), f32),
            pltpu.VMEM((PARTS, 8, LANES), i32),
            pltpu.VMEM((PARTS, 8, LANES), i32),
            pltpu.VMEM((8, PARTS, 2, LANES), f32),
            pltpu.VMEM((TILE, WIDTH), bf16),
            pltpu.VMEM((TILE, WIDTH), bf16),
            pltpu.VMEM((TILE, WIDTH), bf16),
            pltpu.VMEM((31, 32, WIDTH), bf16),
            pltpu.VMEM((8, 32, WIDTH), bf16),
            pltpu.VMEM((8, WIDTH, ROWS), bf16),
            pltpu.VMEM((7, WIDTH, ROWS), bf16),
            pltpu.SemaphoreType.DMA((4,)),
            pltpu.SemaphoreType.DMA((7,)),
            pltpu.SemaphoreType.DMA((7,)),
            pltpu.SemaphoreType.DMA((8,)),
        ],
        compiler_params=pltpu.CompilerParams(
            collective_id=0, has_side_effects=True, vmem_limit_bytes=40 << 20
        ),
        name="attention_backward",
    )(order, segment.reshape(-1, WIDTH), queries, keys, values, grad_out)


def solution(mesh):
    placed = (
        P("head", "ctx", None),
        P("ctx", None),
        P("ctx", None),
        P("head", "ctx", None),
        P(),
        P(),
    )
    return jax.shard_map(
        local,
        mesh=mesh,
        in_specs=placed,
        out_specs=(P("head", "ctx", None), P("ctx", None), P("ctx", None)),
        check_vma=False,
    )
```

time: 904 us -> 64.5 us (0.07)
  blocking collectives: 459 us -> 0 us
  waiting for transfers between devices: 272 us -> 0 us
  matrix products: 137 us -> 0 us
  Pallas kernels: 0 us -> 57.1 us
  between operations: 13.9 us -> 0.65 us
    all_gather x2 -> x0, blocking collectives: 372 us -> none  [the longest x1 189 us: local(): lax.all_gather(stats['lse'], 'ctx', axis=1, tiled=True)]
    all_gather x4 -> x0, waiting for transfers between devices: 269 us -> none  [the longest x1 135 us: local(): lax.all_gather(keys, 'ctx', axis=0, tiled=True)]
    dot_general x112 -> x0, matrix products: 137 us -> none  [the longest x32 36.5 us: key_block(): jnp.einsum('hqd,kd->hqk', queries, block_keys, preferred_element_type=jnp...]
    psum x1 -> x0, blocking collectives: 86.7 us -> none  [local(): grad_k, grad_v = lax.psum((grad_k, grad_v), 'head')]
    pallas_call x0 -> x1, Pallas kernels: none -> 57.1 us  [local(): pl.pallas_call(kernel, out_shape=(jax.ShapeDtypeStruct(queries.shape, bf1...]
  transfers between devices with their start and end apart: 4 -> 0, of which waited for: 2 -> 0; matrix products, arithmetic and copies ran while one was open for 10% -> 0% of each run, Pallas kernels for 0% -> 0%
where the time goes in v1:
time: 64.5 us; the launch traced here: 64 us
  Pallas kernels  57.1 us (89%)
  local copies, waits for them, and re-layouts  6.28 us (10%)
  between operations  0.65 us (1%)
    pallas_call x1, Pallas kernels, local(): pl.pallas_call(kernel, out_shape=(jax.ShapeDtypeStruct(queries.shape, bf1...  57.1 us
    unnamed x15, local copies, waits for them, and re-layouts  6.28 us

profile of v1, /device:TPU:1, one launch (start us, length us, event | category | flops | bytes accessed | tf_op | source)
XLA Modules:
  0.0 64.0 jit_solution(3529736822295709184)
XLA Ops:
  0.6 0.0 copy-start.5
  0.6 0.6 %copy-done.5 = s32[128]{0:T(128)S(1)} copy-done((s32[128]{0:T(128)S(1)}, s32[128]{0:T(128)}, u32[]{:S(2)}) %copy-start.5) | copy-done | bytes 536
  1.3 0.0 copy-start
  1.3 0.8 %copy-done = s32[8192]{0:T(1024)S(1)} copy-done((s32[8192]{0:T(1024)S(1)}, s32[8192]{0:T(1024)}, u32[]{:S(2)}) %copy-start) | copy-done | bytes 32792
  2.0 0.0 copy-start.1
  2.0 0.8 %copy-done.1 = bf16[1,128,128]{2,1,0:T(8,128)(2,1)S(1)} copy-done((bf16[1,128,128]{2,1,0:T(8,128)(2,1)S(1)}, bf16[1,128,128]{2,1,0:T(8,128)(2,1)}, u32[]{:S(2)}) %copy-start.1) | copy-done | bytes 32792
  2.8 0.0 copy-start.2
  2.8 0.8 %copy-done.2 = bf16[128,128]{1,0:T(8,128)(2,1)S(1)} copy-done((bf16[128,128]{1,0:T(8,128)(2,1)S(1)}, bf16[128,128]{1,0:T(8,128)(2,1)}, u32[]{:S(2)}) %copy-start.2) | copy-done | bytes 32792
  3.6 0.0 copy-start.3
  3.6 0.8 %copy-done.3 = bf16[128,128]{1,0:T(8,128)(2,1)S(1)} copy-done((bf16[128,128]{1,0:T(8,128)(2,1)S(1)}, bf16[128,128]{1,0:T(8,128)(2,1)}, u32[]{:S(2)}) %copy-start.3) | copy-done | bytes 32792
  4.3 0.0 copy-start.4
  4.3 0.8 %copy-done.4 = bf16[1,128,128]{2,1,0:T(8,128)(2,1)S(1)} copy-done((bf16[1,128,128]{2,1,0:T(8,128)(2,1)S(1)}, bf16[1,128,128]{2,1,0:T(8,128)(2,1)}, u32[]{:S(2)}) %copy-start.4) | copy-done | bytes 32792
  5.1 57.1 %attention_backward.1 = (bf16[1,128,128]{2,1,0:T(8,128)(2,1)S(1)}, bf16[128,128]{1,0:T(8,128)(2,1)S(1)}, bf16[128,128]{1,0:T(8,128)(2,1)S(1)}) custom-call(s32[128]{0:T(128)S(1)} %copy-done.5, s32[64,128]{1,0:T(8,128)S(1)} %bitcast.1, bf16[1,128,128]{2,1,0:T(8,128)(2,1)S(1)} %copy-done.1, bf16[128,128]{1,0:T(8,128)(2,1)S(1)} %copy-done.2, ...), custom_call_target="tpu_custom_call" | custom-call | tf_op jit(solution)/shard_map/attention_backward/pallas_call | solution.py:312
  62.1 0.6 copy.12
  62.8 0.6 copy.13
  63.4 0.6 copy.14
Async XLA Ops:
  0.6 0.7 %copy-start.5 = (s32[128]{0:T(128)S(1)}, s32[128]{0:T(128)}, u32[]{:S(2)}) copy-start(s32[128]{0:T(128)} %order.1) | copy-start | bytes 1540
  1.3 0.8 %copy-start = (s32[8192]{0:T(1024)S(1)}, s32[8192]{0:T(1024)}, u32[]{:S(2)}) copy-start(s32[8192]{0:T(1024)} %param.11) | copy-start | bytes 98308
  2.0 0.8 %copy-start.1 = (bf16[1,128,128]{2,1,0:T(8,128)(2,1)S(1)}, bf16[1,128,128]{2,1,0:T(8,128)(2,1)}, u32[]{:S(2)}) copy-start(bf16[1,128,128]{2,1,0:T(8,128)(2,1)} %q_in.1) | copy-start | bytes 98308
  2.8 0.8 %copy-start.2 = (bf16[128,128]{1,0:T(8,128)(2,1)S(1)}, bf16[128,128]{1,0:T(8,128)(2,1)}, u32[]{:S(2)}) copy-start(bf16[128,128]{1,0:T(8,128)(2,1)} %k_in.1) | copy-start | bytes 98308
  3.6 0.8 %copy-start.3 = (bf16[128,128]{1,0:T(8,128)(2,1)S(1)}, bf16[128,128]{1,0:T(8,128)(2,1)}, u32[]{:S(2)}) copy-start(bf16[128,128]{1,0:T(8,128)(2,1)} %v_in.1) | copy-start | bytes 98308
  4.3 0.8 %copy-start.4 = (bf16[1,128,128]{2,1,0:T(8,128)(2,1)S(1)}, bf16[1,128,128]{2,1,0:T(8,128)(2,1)}, u32[]{:S(2)}) copy-start(bf16[1,128,128]{2,1,0:T(8,128)(2,1)} %go_in.1) | copy-start | bytes 98308

commit v2 on v1

--- a/solution.py
+++ b/solution.py
@@ -10,6 +10,7 @@
 
 YH, Z, X, YL, CORES = 2, 8, 4, 4, 2
 DOCS = 6
+TOKENS = 8192
 SPAN = 64
 ROWS = 2 * SPAN
 WIDTH = 128
@@ -31,9 +32,9 @@
 
 
 def kernel(
-    order, segment, q_in, k_in, v_in, go_in, dq_out, dk_out, dv_out,
-    qbuf, kv, kbuf, scores, dprobs, pair, peaks, lows, highs, stats,
-    give, take, total, gathered, pieces, dq_part, dq_took,
+    order_in, segment_in, q_in, k_in, v_in, go_in, grads,
+    places, docs, qbuf, kv, kbuf, scores, dprobs, pair, peaks, lows, highs, stats,
+    give, take, kept, total, gathered, pieces, dq_part, dq_took,
     local_sem, send_sem, recv_sem, swap_sem,
 ):
     i, h = lax.axis_index("ctx"), lax.axis_index("head")
@@ -41,27 +42,29 @@
     yl, c = lax.div(h, CORES), lax.rem(h, CORES)
     yp, yj = lax.rem(yl, 2), lax.div(yl, 2)
     own = yp * X + x
+    zs = [lax.rem(z + n, Z) for n in range(Z)]
+    xs = [lax.rem(x + n, X) for n in range(X)]
+    yls = [lax.rem(yl + n, YL) for n in range(YL)]
+    yps, yjs, yhs, cs = (yp, 1 - yp), (yj, 1 - yj), (yh, 1 - yh), (c, 1 - c)
     sibling = device(yh, z, x, yl, 1 - c)
 
     def query_peer(n):
-        tx = lax.rem(x + lax.rem(n, X), X)
-        tp = lax.rem(yp + lax.div(n, X), 2)
+        tx, tp = xs[n % X], yps[n // X]
         return device(yh, z, tx, yj * 2 + tp, c), tp * X + tx
 
     def near_peer(n):
-        return device(yh, lax.rem(z + n, Z), x, yl, c)
+        return device(yh, zs[n], x, yl, c)
 
     def far_peer(n):
-        return device(1 - yh, lax.rem(z + n, Z), x, YL - 1 - yl, c)
+        return device(1 - yh, zs[n], x, YL - 1 - yl, c)
 
     def owner(n):
-        g, dz, jj = lax.div(n, 16), lax.rem(lax.div(n, 2), Z), lax.rem(n, 2)
-        tj = lax.rem(yj + jj, 2)
-        where = device(lax.rem(yh + g, 2), lax.rem(z + Z - dz, Z), x, tj * 2 + yp, c)
-        return where, lax.div(n, 2) * SPAN + tj * 32
+        g, dz, jj = n // 16, n // 2 % Z, n % 2
+        where = device(yhs[g], zs[(Z - dz) % Z], x, yjs[jj] * 2 + yp, c)
+        return where, n // 2 * SPAN + yjs[jj] * 32
 
     def head_peer(n):
-        return device(yh, z, x, lax.rem(yl + lax.div(n, 2), YL), lax.rem(c + n, 2))
+        return device(yh, z, x, yls[n // 2], cs[n % 2])
 
     def remote(src, dst, send, recv, where):
         return pltpu.make_async_remote_copy(
@@ -78,6 +81,10 @@
             return carry
 
         lax.fori_loop(first, last, step, 0)
+
+    def each(first, last, body):
+        for n in range(first, last):
+            body(n)
 
     mine = pl.ds(pl.multiple_of(own * ROWS, ROWS), ROWS)
     loads = [
@@ -85,6 +92,8 @@
         pltpu.make_async_copy(v_in, kv.at[1], local_sem.at[1]),
         pltpu.make_async_copy(q_in.at[0], qbuf.at[0, mine], local_sem.at[2]),
         pltpu.make_async_copy(go_in.at[0], qbuf.at[1, mine], local_sem.at[3]),
+        pltpu.make_async_copy(order_in, places, local_sem.at[4]),
+        pltpu.make_async_copy(segment_in, docs, local_sem.at[5]),
     ]
     for copy in loads:
         copy.start()
@@ -94,10 +103,10 @@
     def greet(where):
         pl.semaphore_signal(barrier, inc=1, device_id=where, device_id_type=MESH)
 
-    loop(1, 32, lambda n: greet(owner(n)[0]))
-    loop(0, 8, lambda n: greet(far_peer(n)))
-    loop(1, 8, lambda n: greet(query_peer(n)[0]))
-    loop(1, 8, lambda n: greet(head_peer(n)))
+    each(1, 32, lambda n: greet(owner(n)[0]))
+    each(0, 8, lambda n: greet(far_peer(n)))
+    each(1, 8, lambda n: greet(query_peer(n)[0]))
+    each(1, 8, lambda n: greet(head_peer(n)))
 
     for copy in loads:
         copy.wait()
@@ -108,28 +117,28 @@
     pl.semaphore_wait(barrier, 31 + 8 + 7 + 7)
 
     def send_far(n):
-        rows = pl.ds(pl.multiple_of(512 + n * SPAN, SPAN), SPAN)
+        rows = pl.ds(512 + n * SPAN, SPAN)
         remote(kv.at[c, other], kbuf.at[c, rows], send_sem.at[0], recv_sem.at[1], far_peer(n)).start()
 
     def send_near(n):
-        rows = pl.ds(pl.multiple_of(n * SPAN, SPAN), SPAN)
+        rows = pl.ds(n * SPAN, SPAN)
         remote(kv.at[c, half], kbuf.at[c, rows], send_sem.at[0], recv_sem.at[0], near_peer(n)).start()
 
     def send_query(n):
         remote(qbuf.at[:, mine], qbuf.at[:, mine], send_sem.at[1], recv_sem.at[2], query_peer(n)[0]).start()
 
-    loop(0, 8, send_far)
-    loop(1, 8, send_near)
-    loop(1, 8, send_query)
-
-    docs = segment[...]
+    each(0, 8, send_far)
+    each(1, 8, send_near)
+    each(1, 8, send_query)
+
+    doc = docs[...]
     starts = [
-        jnp.sum((docs < d).astype(jnp.int32), axis=(0, 1), keepdims=True) for d in range(1, DOCS)
+        jnp.sum((doc < d).astype(jnp.int32), axis=(0, 1), keepdims=True) for d in range(1, DOCS)
     ]
     lane = lax.broadcasted_iota(jnp.int32, (8, ROWS), 1)
     for s in range(X):
         ctx = yh * (Z * X) + z * X + s
-        first, second = order[2 * ctx], order[2 * ctx + 1]
+        first, second = places[2 * ctx], places[2 * ctx + 1]
         place = jnp.where(lane < SPAN, first * SPAN + lane, second * SPAN + lane - SPAN)
         low = jnp.zeros_like(place)
         for start in starts:
@@ -159,7 +168,7 @@
         peak = None if g == 0 else peaks[t]
         for n in range(8):
             ctx = lax.rem(yh + g, 2) * (Z * X) + lax.rem(z + Z - n, Z) * X + x
-            place = order[2 * ctx + yp] * SPAN + row
+            place = places[2 * ctx + yp] * SPAN + row
             masked = jnp.where(
                 (place >= low) & (place <= high), s[n * SPAN : n * SPAN + SPAN], NEGATIVE
             )
@@ -201,44 +210,60 @@
     def send_stats(n):
         remote(stats.at[0], stats.at[n], send_sem.at[2], recv_sem.at[3], query_peer(n)[0]).start()
 
-    loop(1, 8, send_stats)
+    each(1, 8, send_stats)
     wait_for(stats.at[pl.ds(1, 7)], recv_sem.at[3])
 
-    def differentiate(t):
+    def combine(t):
         every = [stats[n, t, 0:1] for n in range(8)]
         top = functools.reduce(jnp.maximum, every)
         shares = [jnp.exp2(e - top) for e in every]
         mass = functools.reduce(jnp.add, shares)
         delta = functools.reduce(jnp.add, [s * stats[n, t, 1:2] for n, s in enumerate(shares)]) / mass
         factor = jnp.exp2(peaks[t, 0:1] - top) / mass
-
-        def step(r, carry):
-            rows = pl.ds(pl.multiple_of(r * CHUNK, CHUNK), CHUNK)
-            probs = scores[t, rows] * factor
+        peaks[t, 0:1] = factor
+        peaks[t, 1:2] = delta
+
+    loop(0, PARTS, combine)
+
+    def differentiate(r):
+        def step(n):
+            t = lax.div(n, 2)
+            rows = pl.ds(pl.multiple_of(r * LANES + lax.rem(n, 2) * CHUNK, CHUNK), CHUNK)
+            probs = scores[t, rows] * peaks[t, 0:1]
             pair[1, t, rows] = probs.astype(jnp.bfloat16)
-            pair[0, t, rows] = (probs * (dprobs[t, rows] - delta) * SCALE).astype(jnp.bfloat16)
-            return carry
-
-        lax.fori_loop(0, TILE // CHUNK, step, 0)
-
-    loop(0, PARTS, differentiate)
-
-    def key_side(which, r):
-        rows = pl.ds(pl.multiple_of(r * LANES, LANES), LANES)
+            pair[0, t, rows] = (probs * (dprobs[t, rows] - peaks[t, 1:2]) * SCALE).astype(jnp.bfloat16)
+
+        loop(0, 2 * PARTS, step)
+
+    def key_side(which, rows):
         acc = jnp.zeros((LANES, WIDTH), jnp.float32)
         for t in range(PARTS):
             acc += jnp.dot(
                 pair[which, t, rows], qbuf[which, t * LANES : t * LANES + LANES],
                 preferred_element_type=jnp.float32,
             )
-        return acc, rows
-
-    def give_away(r):
-        acc, rows = key_side(1 - c, r)
-        give[rows] = acc.astype(jnp.bfloat16)
+        return acc
+
+    def send_piece(n):
+        where, first = owner(n)
+        rows = pl.ds(pl.multiple_of(first, 32), 32)
+        remote(total.at[rows], gathered.at[n - 1], send_sem.at[5], recv_sem.at[5], where).start()
+
+    def settle(r):
+        rows = pl.ds(r * LANES, LANES)
+        wait_for(take.at[rows], swap_sem.at[4 + r])
+        total[rows] = (kept[rows] + take[rows].astype(jnp.float32)).astype(jnp.bfloat16)
+        each(max(1, 8 * r), 8 * r + 8, send_piece)
+
+    for r in (3, 2, 1, 0):
+        rows = pl.ds(r * LANES, LANES)
+        differentiate(r)
+        give[rows] = key_side(1 - c, rows).astype(jnp.bfloat16)
         remote(give.at[rows], take.at[rows], send_sem.at[3], swap_sem.at[4 + r], sibling).start()
-
-    loop(0, 4, give_away)
+        kept[rows] = key_side(c, rows)
+        if r < 3:
+            settle(r + 1)
+    settle(0)
 
     def query_side(t):
         part = lax.dot_general(kbuf[0], pair[0, t], TN, preferred_element_type=jnp.float32)
@@ -252,26 +277,13 @@
         where, slot = query_peer(n)
         remote(dq_part.at[slot], dq_took.at[n - 1], send_sem.at[4], recv_sem.at[4], where).start()
 
-    loop(1, 8, send_dq)
-
-    def send_piece(n):
-        where, first = owner(n)
-        rows = pl.ds(pl.multiple_of(first, 32), 32)
-        remote(total.at[rows], gathered.at[n - 1], send_sem.at[5], recv_sem.at[5], where).start()
-
-    def keep(r):
-        acc, rows = key_side(c, r)
-        wait_for(take.at[rows], swap_sem.at[4 + r])
-        total[rows] = (acc + take[rows].astype(jnp.float32)).astype(jnp.bfloat16)
-        loop(jnp.where(r == 0, 1, 8 * r), 8 * r + 8, send_piece)
-
-    loop(0, 4, keep)
+    each(1, 8, send_dq)
 
     wait_for(dq_took, recv_sem.at[4])
     dq = dq_part[own].astype(jnp.float32)
     for n in range(7):
         dq += dq_took[n].astype(jnp.float32)
-    dq_out[0] = dq.T.astype(jnp.bfloat16)
+    grads[0] = dq.T.astype(jnp.bfloat16)
 
     first = pl.ds(pl.multiple_of(yj * 32, 32), 32)
     wait_for(gathered, recv_sem.at[5])
@@ -283,13 +295,13 @@
     def send_result(n):
         remote(pieces.at[0], pieces.at[n], send_sem.at[6], recv_sem.at[6], head_peer(n)).start()
 
-    loop(1, 8, send_result)
+    each(1, 8, send_result)
     wait_for(pieces.at[pl.ds(1, 7)], recv_sem.at[6])
     for n in range(YL):
         fl = lax.rem(yl + YL - n, YL)
         rows = pl.ds(pl.multiple_of(lax.rem(fl, 2) * SPAN + lax.div(fl, 2) * 32, 32), 32)
-        dk_out[rows] = pieces[2 * n + c]
-        dv_out[rows] = pieces[2 * n + 1 - c]
+        grads[1, rows] = pieces[2 * n + c]
+        grads[2, rows] = pieces[2 * n + 1 - c]
 
     wait_for(kbuf.at[0, pl.ds(0, 960)], send_sem.at[0])
     wait_for(qbuf.at[:, pl.ds(ROWS, 7 * ROWS)], send_sem.at[1])
@@ -304,21 +316,15 @@
 
 def local(queries, keys, values, grad_out, order, segment):
     bf16, f32, i32 = jnp.bfloat16, jnp.float32, jnp.int32
-    smem, vmem, hbm = (
-        pl.BlockSpec(memory_space=pltpu.SMEM),
-        pl.BlockSpec(memory_space=pltpu.VMEM),
-        pl.BlockSpec(memory_space=pl.ANY),
-    )
-    return pl.pallas_call(
+    vmem, hbm = pl.BlockSpec(memory_space=pltpu.VMEM), pl.BlockSpec(memory_space=pltpu.HBM)
+    grads = pl.pallas_call(
         kernel,
-        out_shape=(
-            jax.ShapeDtypeStruct(queries.shape, bf16),
-            jax.ShapeDtypeStruct(keys.shape, bf16),
-            jax.ShapeDtypeStruct(values.shape, bf16),
-        ),
-        in_specs=[smem, vmem, hbm, hbm, hbm, hbm],
-        out_specs=(vmem, vmem, vmem),
+        out_shape=jax.ShapeDtypeStruct((3, ROWS, WIDTH), bf16),
+        in_specs=[hbm] * 6,
+        out_specs=vmem,
         scratch_shapes=[
+            pltpu.SMEM((TOKENS // SPAN,), i32),
+            pltpu.VMEM((TOKENS // WIDTH, WIDTH), i32),
             pltpu.VMEM((2, TILE, WIDTH), bf16),
             pltpu.VMEM((2, ROWS, WIDTH), bf16),
             pltpu.VMEM((2, TILE, WIDTH), bf16),
@@ -331,21 +337,23 @@
             pltpu.VMEM((8, PARTS, 2, LANES), f32),
             pltpu.VMEM((TILE, WIDTH), bf16),
             pltpu.VMEM((TILE, WIDTH), bf16),
+            pltpu.VMEM((TILE, WIDTH), f32),
             pltpu.VMEM((TILE, WIDTH), bf16),
             pltpu.VMEM((31, 32, WIDTH), bf16),
             pltpu.VMEM((8, 32, WIDTH), bf16),
             pltpu.VMEM((8, WIDTH, ROWS), bf16),
             pltpu.VMEM((7, WIDTH, ROWS), bf16),
-            pltpu.SemaphoreType.DMA((4,)),
+            pltpu.SemaphoreType.DMA((6,)),
             pltpu.SemaphoreType.DMA((7,)),
             pltpu.SemaphoreType.DMA((7,)),
             pltpu.SemaphoreType.DMA((8,)),
         ],
         compiler_params=pltpu.CompilerParams(
-            collective_id=0, has_side_effects=True, vmem_limit_bytes=40 << 20
+            collective_id=0, has_side_effects=True, vmem_limit_bytes=63 << 20
         ),
         name="attention_backward",
     )(order, segment.reshape(-1, WIDTH), queries, keys, values, grad_out)
+    return grads[0:1], grads[1], grads[2]
 
 
 def solution(mesh):

time: 64.5 us -> 55.6 us (0.86)
  local copies, waits for them, and re-layouts: 6.28 us -> 1.43 us
  Pallas kernels: 57.1 us -> 53.3 us
    unnamed x15 -> x0, local copies, waits for them, and re-layouts: 6.28 us -> none
    pallas_call x1, Pallas kernels: 57.1 us -> 53.3 us  [local(): pl.pallas_call(kernel, out_shape=jax.ShapeDtypeStruct((3, ROWS, WIDTH), b...]
    squeeze x0 -> x1, local copies, waits for them, and re-layouts: none -> 1.43 us  [local(): return (grads[0:1], grads[1], grads[2])]
where the time goes in v2:
time: 55.6 us; the launch traced here: 55.3 us
  Pallas kernels  53.3 us (96%)
  local copies, waits for them, and re-layouts  1.43 us (3%)
  between operations  0.64 us (1%)
    pallas_call x1, Pallas kernels, local(): pl.pallas_call(kernel, out_shape=jax.ShapeDtypeStruct((3, ROWS, WIDTH), b...  53.3 us
    squeeze x1, local copies, waits for them, and re-layouts, local(): return (grads[0:1], grads[1], grads[2])  1.43 us

profile of v2, /device:TPU:1, one launch (start us, length us, event | category | flops | bytes accessed | tf_op | source)
XLA Modules:
  0.0 55.3 jit_solution(7280851385756183349)
XLA Ops:
  0.6 53.3 %attention_backward.1 = bf16[3,128,128]{2,1,0:T(8,128)(2,1)} custom-call(s32[128]{0:T(128)} %order_in.1, s32[64,128]{1,0:T(8,128)} %bitcast.5, bf16[1,128,128]{2,1,0:T(8,128)(2,1)} %q_in.1, bf16[128,128]{1,0:T(8,128)(2,1)} %k_in.1, bf16[128,128]{1,0:T(8,128)(2,1)} %v_in.1, bf16[1,128,128]{2,1,0:T(8,128)(2,1)} %go_in.1), custom_call_target="tpu_custom_call" | custom-call | tf_op jit(solution)/shard_map/attention_backward/pallas_call | solution.py:320
  53.9 1.4 %slice_bitcast_fusion = (bf16[128,128]{1,0:T(8,128)(2,1)}, bf16[128,128]{1,0:T(8,128)(2,1)}, bf16[1,128,128]{2,1,0:T(8,128)(2,1)}) fusion(bf16[3,128,128]{2,1,0:T(8,128)(2,1)} %attention_backward.1), kind=kLoop, calls=%fused_computation | loop fusion | bytes 196608 | tf_op jit(solution)/shard_map/squeeze | solution.py:356

commit v3 on v2

--- a/solution.py
+++ b/solution.py
@@ -33,9 +33,9 @@
 
 def kernel(
     order_in, segment_in, q_in, k_in, v_in, go_in, grads,
-    places, docs, qbuf, kv, kbuf, scores, dprobs, pair, peaks, lows, highs, stats,
-    give, take, kept, total, gathered, pieces, dq_part, dq_took,
-    local_sem, send_sem, recv_sem, swap_sem,
+    places, docs, qbuf, kv, kbuf, scores, dprobs, pair, peaks, masses, weights, lows, highs,
+    logs, deltas, give, take, kept, total, gathered, pieces, dq_part, dq_took,
+    local_sem, send_sem, recv_sem, swap_sem, take_sem,
 ):
     i, h = lax.axis_index("ctx"), lax.axis_index("head")
     yh, z, x = lax.div(i, Z * X), lax.rem(lax.div(i, X), Z), lax.rem(i, X)
@@ -59,7 +59,7 @@
         return device(1 - yh, zs[n], x, YL - 1 - yl, c)
 
     def owner(n):
-        g, dz, jj = n // 16, n // 2 % Z, n % 2
+        g, dz, jj = n // 16, n // 2 % 4 * 2 + n // 8 % 2, n % 2
         where = device(yhs[g], zs[(Z - dz) % Z], x, yjs[jj] * 2 + yp, c)
         return where, n // 2 * SPAN + yjs[jj] * 32
 
@@ -112,24 +112,42 @@
         copy.wait()
     half = pl.ds(pl.multiple_of(yp * SPAN, SPAN), SPAN)
     other = pl.ds(pl.multiple_of((1 - yp) * SPAN, SPAN), SPAN)
-    kbuf[:, :SPAN] = kv[:, half]
 
     pl.semaphore_wait(barrier, 31 + 8 + 7 + 7)
 
-    def send_far(n):
-        rows = pl.ds(512 + n * SPAN, SPAN)
-        remote(kv.at[c, other], kbuf.at[c, rows], send_sem.at[0], recv_sem.at[1], far_peer(n)).start()
-
-    def send_near(n):
-        rows = pl.ds(n * SPAN, SPAN)
-        remote(kv.at[c, half], kbuf.at[c, rows], send_sem.at[0], recv_sem.at[0], near_peer(n)).start()
-
-    def send_query(n):
-        remote(qbuf.at[:, mine], qbuf.at[:, mine], send_sem.at[1], recv_sem.at[2], query_peer(n)[0]).start()
-
-    each(0, 8, send_far)
-    each(1, 8, send_near)
-    each(1, 8, send_query)
+    def send_far(a, m):
+        rows = pl.ds(pl.multiple_of(512 + c * 256 + m * SPAN, SPAN), SPAN)
+        where = device(1 - yh, lax.rem(z + 2 * m + c, Z), x, YL - 1 - yl, c)
+        remote(kv.at[a, other], kbuf.at[a, rows], send_sem.at[0], recv_sem.at[2 * a + 1], where).start()
+
+    def send_near(a, m):
+        rows = pl.ds(pl.multiple_of(c * 256 + m * SPAN, SPAN), SPAN)
+        where = device(yh, lax.rem(z + 2 * m + c, Z), x, yl, c)
+
+        def send():
+            remote(kv.at[a, half], kbuf.at[a, rows], send_sem.at[0], recv_sem.at[2 * a], where).start()
+
+        if m > 0:
+            send()
+            return
+        pl.when(c == 1)(send)
+
+        @pl.when(c == 0)
+        def _():
+            pltpu.make_async_copy(kv.at[a, half], kbuf.at[a, pl.ds(0, SPAN)], recv_sem.at[2 * a]).start()
+
+    def send_query(a, n):
+        remote(
+            qbuf.at[a, mine], qbuf.at[a, mine], send_sem.at[1], recv_sem.at[4 + a], query_peer(n)[0]
+        ).start()
+
+    for a in range(2):
+        for m in range(4):
+            send_far(a, m)
+        for m in range(4):
+            send_near(a, m)
+        for n in range(1, 8):
+            send_query(a, n)
 
     doc = docs[...]
     starts = [
@@ -147,15 +165,18 @@
             lows[t // 2, :, (t % 2) * ROWS : (t % 2 + 1) * ROWS] = low
             highs[t // 2, :, (t % 2) * ROWS : (t % 2 + 1) * ROWS] = place
 
-    wait_for(kbuf.at[0, pl.ds(SPAN, 448)], recv_sem.at[0])
-    near = kbuf.at[c, pl.ds(SPAN, 448)]
-    swap_near = remote(near, near, swap_sem.at[0], swap_sem.at[1], sibling)
-    swap_near.start()
-    wait_for(kbuf.at[0, pl.ds(512, 512)], recv_sem.at[1])
-    far = kbuf.at[c, pl.ds(512, 512)]
-    swap_far = remote(far, far, swap_sem.at[2], swap_sem.at[3], sibling)
-    swap_far.start()
-    wait_for(qbuf.at[:, pl.ds(ROWS, 7 * ROWS)], recv_sem.at[2])
+    def hand_over(a, g):
+        rows = pl.ds(pl.multiple_of(g * 512 + c * 256, 256), 256)
+        wait_for(kbuf.at[a, rows], recv_sem.at[2 * a + g])
+        remote(kbuf.at[a, rows], kbuf.at[a, rows], swap_sem.at[4], swap_sem.at[2 * a + g], sibling).start()
+
+    def handed(a, g):
+        rows = pl.ds(pl.multiple_of(g * 512 + (1 - c) * 256, 256), 256)
+        wait_for(kbuf.at[a, rows], swap_sem.at[2 * a + g])
+
+    hand_over(0, 0)
+    hand_over(0, 1)
+    wait_for(qbuf.at[0, pl.ds(ROWS, 7 * ROWS)], recv_sem.at[4])
 
     row = lax.broadcasted_iota(jnp.int32, (SPAN, LANES), 0)
 
@@ -167,7 +188,8 @@
         )
         peak = None if g == 0 else peaks[t]
         for n in range(8):
-            ctx = lax.rem(yh + g, 2) * (Z * X) + lax.rem(z + Z - n, Z) * X + x
+            behind = zs[(Z - (n % 4 * 2 + n // 4)) % Z]
+            ctx = yhs[g] * (Z * X) + behind * X + x
             place = places[2 * ctx + yp] * SPAN + row
             masked = jnp.where(
                 (place >= low) & (place <= high), s[n * SPAN : n * SPAN + SPAN], NEGATIVE
@@ -176,17 +198,13 @@
             top = jnp.max(masked.reshape(SPAN // 8, 8, LANES), axis=0)
             peak = top if peak is None else jnp.maximum(peak, top)
         peaks[t] = peak
-        dprobs[t, g * 512 : g * 512 + 512] = lax.dot_general(
-            kbuf[1, g * 512 : g * 512 + 512], qbuf[1, rows], NT, preferred_element_type=jnp.float32
-        )
-
-    swap_near.wait_recv()
+
+    handed(0, 0)
     loop(0, PARTS, functools.partial(product, 0))
-    swap_far.wait_recv()
+    handed(0, 1)
     loop(0, PARTS, functools.partial(product, 1))
-
-    def summed(a):
-        return jnp.sum(a.reshape(CHUNK // 8, 8, LANES), axis=0)
+    hand_over(1, 0)
+    hand_over(1, 1)
 
     def weigh(t):
         peak = jnp.maximum(jnp.max(peaks[t], axis=0, keepdims=True), FLOOR)
@@ -195,42 +213,74 @@
             rows = pl.ds(pl.multiple_of(r * CHUNK, CHUNK), CHUNK)
             expo = jnp.exp2((scores[t, rows] - peak) * (SCALE * LOG2E))
             scores[t, rows] = expo
-            return carry[0] + summed(expo), carry[1] + summed(expo * dprobs[t, rows])
-
-        zero = jnp.zeros((8, LANES), jnp.float32)
-        mass, weighted = lax.fori_loop(0, TILE // CHUNK, step, (zero, zero))
+            return carry + jnp.sum(expo.reshape(CHUNK // 8, 8, LANES), axis=0)
+
+        mass = lax.fori_loop(0, TILE // CHUNK, step, jnp.zeros((8, LANES), jnp.float32))
         mass = jnp.maximum(jnp.sum(mass, axis=0, keepdims=True), 1e-30)
-        weighted = jnp.sum(weighted, axis=0, keepdims=True)
-        peaks[t] = jnp.broadcast_to(peak * (SCALE * LOG2E), (8, LANES))
-        stats[0, t, 0:1] = peak * (SCALE * LOG2E) + jnp.log2(mass)
-        stats[0, t, 1:2] = weighted / mass
+        peak = peak * (SCALE * LOG2E)
+        peaks[t, 0:1] = peak
+        masses[t] = mass
+        logs[0, t] = peak + jnp.log2(mass)
 
     loop(0, PARTS, weigh)
 
-    def send_stats(n):
-        remote(stats.at[0], stats.at[n], send_sem.at[2], recv_sem.at[3], query_peer(n)[0]).start()
-
-    each(1, 8, send_stats)
-    wait_for(stats.at[pl.ds(1, 7)], recv_sem.at[3])
-
-    def combine(t):
-        every = [stats[n, t, 0:1] for n in range(8)]
+    def send_logs(n):
+        remote(logs.at[0], logs.at[n], send_sem.at[2], recv_sem.at[6], query_peer(n)[0]).start()
+
+    each(1, 8, send_logs)
+
+    def cotangent(g, t):
+        rows = pl.ds(pl.multiple_of(t * LANES, LANES), LANES)
+        d = lax.dot_general(
+            kbuf[1, g * 512 : g * 512 + 512], qbuf[1, rows], NT, preferred_element_type=jnp.float32
+        )
+        dprobs[t, g * 512 : g * 512 + 512] = d
+        weighted = jnp.sum((scores[t, g * 512 : g * 512 + 512] * d).reshape(64, 8, LANES), axis=0)
+        if g == 0:
+            weights[t] = weighted
+        else:
+            weighted = jnp.sum(weights[t] + weighted, axis=0, keepdims=True)
+            deltas[0, t] = weighted / masses[t]
+
+    wait_for(qbuf.at[1, pl.ds(ROWS, 7 * ROWS)], recv_sem.at[5])
+    handed(1, 0)
+    loop(0, PARTS, functools.partial(cotangent, 0))
+    handed(1, 1)
+    loop(0, PARTS, functools.partial(cotangent, 1))
+
+    def send_deltas(n):
+        remote(deltas.at[0], deltas.at[n], send_sem.at[7], recv_sem.at[7], query_peer(n)[0]).start()
+
+    each(1, 8, send_deltas)
+
+    def lse_of(t):
+        every = [logs[n, t] for n in range(8)]
         top = functools.reduce(jnp.maximum, every)
         shares = [jnp.exp2(e - top) for e in every]
-        mass = functools.reduce(jnp.add, shares)
-        delta = functools.reduce(jnp.add, [s * stats[n, t, 1:2] for n, s in enumerate(shares)]) / mass
-        factor = jnp.exp2(peaks[t, 0:1] - top) / mass
-        peaks[t, 0:1] = factor
-        peaks[t, 1:2] = delta
-
-    loop(0, PARTS, combine)
-
-    def differentiate(r):
+        return top, shares, functools.reduce(jnp.add, shares)
+
+    def normalize(t):
+        top, _, mass = lse_of(t)
+        peaks[t, 0:1] = jnp.exp2(peaks[t, 0:1] - top) / mass
+
+    def center(t):
+        _, shares, mass = lse_of(t)
+        peaks[t, 1:2] = functools.reduce(jnp.add, [s * deltas[n, t] for n, s in enumerate(shares)]) / mass
+
+    def place_of(r, n):
+        return lax.div(n, 2), pl.ds(pl.multiple_of(r * LANES + lax.rem(n, 2) * CHUNK, CHUNK), CHUNK)
+
+    def value_weights(r):
         def step(n):
-            t = lax.div(n, 2)
-            rows = pl.ds(pl.multiple_of(r * LANES + lax.rem(n, 2) * CHUNK, CHUNK), CHUNK)
+            t, rows = place_of(r, n)
+            pair[1, t, rows] = (scores[t, rows] * peaks[t, 0:1]).astype(jnp.bfloat16)
+
+        loop(0, 2 * PARTS, step)
+
+    def key_weights(r):
+        def step(n):
+            t, rows = place_of(r, n)
             probs = scores[t, rows] * peaks[t, 0:1]
-            pair[1, t, rows] = probs.astype(jnp.bfloat16)
             pair[0, t, rows] = (probs * (dprobs[t, rows] - peaks[t, 1:2]) * SCALE).astype(jnp.bfloat16)
 
         loop(0, 2 * PARTS, step)
@@ -247,23 +297,39 @@
     def send_piece(n):
         where, first = owner(n)
         rows = pl.ds(pl.multiple_of(first, 32), 32)
-        remote(total.at[rows], gathered.at[n - 1], send_sem.at[5], recv_sem.at[5], where).start()
+        remote(total.at[rows], gathered.at[n - 1], send_sem.at[5], recv_sem.at[9], where).start()
 
     def settle(r):
         rows = pl.ds(r * LANES, LANES)
-        wait_for(take.at[rows], swap_sem.at[4 + r])
+        wait_for(take.at[rows], take_sem.at[r])
         total[rows] = (kept[rows] + take[rows].astype(jnp.float32)).astype(jnp.bfloat16)
         each(max(1, 8 * r), 8 * r + 8, send_piece)
 
-    for r in (3, 2, 1, 0):
-        rows = pl.ds(r * LANES, LANES)
-        differentiate(r)
-        give[rows] = key_side(1 - c, rows).astype(jnp.bfloat16)
-        remote(give.at[rows], take.at[rows], send_sem.at[3], swap_sem.at[4 + r], sibling).start()
-        kept[rows] = key_side(c, rows)
-        if r < 3:
-            settle(r + 1)
-    settle(0)
+    def one_side(which, weigh_chunk):
+        keeps = c == which
+        for r in (3, 2, 1, 0):
+            rows = pl.ds(r * LANES, LANES)
+            weigh_chunk(r)
+            acc = key_side(which, rows)
+
+            @pl.when(jnp.logical_not(keeps))
+            def _():
+                give[rows] = acc.astype(jnp.bfloat16)
+                remote(give.at[rows], take.at[rows], send_sem.at[3], take_sem.at[r], sibling).start()
+
+            @pl.when(keeps)
+            def _():
+                kept[rows] = acc
+                if r < 3:
+                    settle(r + 1)
+        pl.when(keeps)(lambda: settle(0))
+
+    wait_for(logs.at[pl.ds(1, 7)], recv_sem.at[6])
+    loop(0, PARTS, normalize)
+    one_side(1, value_weights)
+    wait_for(deltas.at[pl.ds(1, 7)], recv_sem.at[7])
+    loop(0, PARTS, center)
+    one_side(0, key_weights)
 
     def query_side(t):
         part = lax.dot_general(kbuf[0], pair[0, t], TN, preferred_element_type=jnp.float32)
@@ -275,39 +341,40 @@
 
     def send_dq(n):
         where, slot = query_peer(n)
-        remote(dq_part.at[slot], dq_took.at[n - 1], send_sem.at[4], recv_sem.at[4], where).start()
+        remote(dq_part.at[slot], dq_took.at[n - 1], send_sem.at[4], recv_sem.at[8], where).start()
 
     each(1, 8, send_dq)
 
-    wait_for(dq_took, recv_sem.at[4])
+    wait_for(dq_took, recv_sem.at[8])
     dq = dq_part[own].astype(jnp.float32)
     for n in range(7):
         dq += dq_took[n].astype(jnp.float32)
     grads[0] = dq.T.astype(jnp.bfloat16)
 
     first = pl.ds(pl.multiple_of(yj * 32, 32), 32)
-    wait_for(gathered, recv_sem.at[5])
+    wait_for(gathered, recv_sem.at[9])
     result = total[first].astype(jnp.float32)
     for n in range(31):
         result += gathered[n].astype(jnp.float32)
     pieces[0] = result.astype(jnp.bfloat16)
 
     def send_result(n):
-        remote(pieces.at[0], pieces.at[n], send_sem.at[6], recv_sem.at[6], head_peer(n)).start()
+        remote(pieces.at[0], pieces.at[n], send_sem.at[6], recv_sem.at[10], head_peer(n)).start()
 
     each(1, 8, send_result)
-    wait_for(pieces.at[pl.ds(1, 7)], recv_sem.at[6])
+    wait_for(pieces.at[pl.ds(1, 7)], recv_sem.at[10])
     for n in range(YL):
         fl = lax.rem(yl + YL - n, YL)
         rows = pl.ds(pl.multiple_of(lax.rem(fl, 2) * SPAN + lax.div(fl, 2) * 32, 32), 32)
         grads[1, rows] = pieces[2 * n + c]
         grads[2, rows] = pieces[2 * n + 1 - c]
 
-    wait_for(kbuf.at[0, pl.ds(0, 960)], send_sem.at[0])
+    pl.when(c == 0)(lambda: wait_for(kbuf.at[0, pl.ds(0, 896)], send_sem.at[0]))
+    pl.when(c == 1)(lambda: wait_for(kbuf.at[0], send_sem.at[0]))
     wait_for(qbuf.at[:, pl.ds(ROWS, 7 * ROWS)], send_sem.at[1])
-    swap_near.wait_send()
-    swap_far.wait_send()
-    wait_for(stats.at[pl.ds(1, 7)], send_sem.at[2])
+    wait_for(kbuf.at[0], swap_sem.at[4])
+    wait_for(logs.at[pl.ds(1, 7)], send_sem.at[2])
+    wait_for(deltas.at[pl.ds(1, 7)], send_sem.at[7])
     wait_for(give, send_sem.at[3])
     wait_for(dq_took, send_sem.at[4])
     wait_for(gathered, send_sem.at[5])
@@ -319,7 +386,7 @@
     vmem, hbm = pl.BlockSpec(memory_space=pltpu.VMEM), pl.BlockSpec(memory_space=pltpu.HBM)
     grads = pl.pallas_call(
         kernel,
-        out_shape=jax.ShapeDtypeStruct((3, ROWS, WIDTH), bf16),
+        out_shape=pltpu.VMEM((3, ROWS, WIDTH), bf16),
         in_specs=[hbm] * 6,
         out_specs=vmem,
         scratch_shapes=[
@@ -332,9 +399,12 @@
             pltpu.VMEM((PARTS, TILE, LANES), f32),
             pltpu.VMEM((2, PARTS, TILE, LANES), bf16),
             pltpu.VMEM((PARTS, 8, LANES), f32),
+            pltpu.VMEM((PARTS, 1, LANES), f32),
+            pltpu.VMEM((PARTS, 8, LANES), f32),
             pltpu.VMEM((PARTS, 8, LANES), i32),
             pltpu.VMEM((PARTS, 8, LANES), i32),
-            pltpu.VMEM((8, PARTS, 2, LANES), f32),
+            pltpu.VMEM((8, PARTS, 1, LANES), f32),
+            pltpu.VMEM((8, PARTS, 1, LANES), f32),
             pltpu.VMEM((TILE, WIDTH), bf16),
             pltpu.VMEM((TILE, WIDTH), bf16),
             pltpu.VMEM((TILE, WIDTH), f32),
@@ -344,12 +414,13 @@
             pltpu.VMEM((8, WIDTH, ROWS), bf16),
             pltpu.VMEM((7, WIDTH, ROWS), bf16),
             pltpu.SemaphoreType.DMA((6,)),
-            pltpu.SemaphoreType.DMA((7,)),
-            pltpu.SemaphoreType.DMA((7,)),
             pltpu.SemaphoreType.DMA((8,)),
+            pltpu.SemaphoreType.DMA((11,)),
+            pltpu.SemaphoreType.DMA((5,)),
+            pltpu.SemaphoreType.DMA((4,)),
         ],
         compiler_params=pltpu.CompilerParams(
-            collective_id=0, has_side_effects=True, vmem_limit_bytes=63 << 20
+            collective_id=0, has_side_effects=True, vmem_limit_bytes=55 << 20
         ),
         name="attention_backward",
     )(order, segment.reshape(-1, WIDTH), queries, keys, values, grad_out)

time: 55.6 us -> 53.6 us (0.964)
  Pallas kernels: 53.3 us -> 52.1 us
  local copies, waits for them, and re-layouts: 1.43 us -> 0.64 us
    pallas_call x1, Pallas kernels: 53.3 us -> 52.1 us  [local(): pl.pallas_call(kernel, out_shape=pltpu.VMEM((3, ROWS, WIDTH), bf16), in_s...]
    squeeze x1, local copies, waits for them, and re-layouts: 1.43 us -> 0.64 us  [local(): return (grads[0:1], grads[1], grads[2])]
where the time goes in v3:
time: 53.6 us; the launch traced here: 53.4 us
  Pallas kernels  52.1 us (97%)
  local copies, waits for them, and re-layouts  0.64 us (1%)
  between operations  0.64 us (1%)
    pallas_call x1, Pallas kernels, local(): pl.pallas_call(kernel, out_shape=pltpu.VMEM((3, ROWS, WIDTH), bf16), in_s...  52.1 us

profile of v3, /device:TPU:1, one launch (start us, length us, event | category | flops | bytes accessed | tf_op | source)
XLA Modules:
  0.0 53.4 jit_solution(3321448920115737170)
XLA Ops:
  0.6 52.1 %attention_backward.1 = bf16[3,128,128]{2,1,0:T(8,128)(2,1)S(1)} custom-call(s32[128]{0:T(128)} %order_in.1, s32[64,128]{1,0:T(8,128)} %bitcast.5, bf16[1,128,128]{2,1,0:T(8,128)(2,1)} %q_in.1, bf16[128,128]{1,0:T(8,128)(2,1)} %k_in.1, bf16[128,128]{1,0:T(8,128)(2,1)} %v_in.1, bf16[1,128,128]{2,1,0:T(8,128)(2,1)} %go_in.1), custom_call_target="tpu_custom_call" | custom-call | tf_op jit(solution)/shard_map/attention_backward/pallas_call | solution.py:387
  52.8 0.6 %slice_bitcast_fusion = (bf16[128,128]{1,0:T(8,128)(2,1)}, bf16[128,128]{1,0:T(8,128)(2,1)}, bf16[1,128,128]{2,1,0:T(8,128)(2,1)}) fusion(bf16[3,128,128]{2,1,0:T(8,128)(2,1)S(1)} %attention_backward.1), kind=kLoop, calls=%fused_computation | loop fusion | bytes 196608 | tf_op jit(solution)/shard_map/squeeze | solution.py:427

commit v4 on v3

--- a/solution.py
+++ b/solution.py
@@ -12,6 +12,7 @@
 DOCS = 6
 TOKENS = 8192
 SPAN = 64
+HALF = SPAN // 2
 ROWS = 2 * SPAN
 WIDTH = 128
 TILE = 1024
@@ -34,7 +35,7 @@
 def kernel(
     order_in, segment_in, q_in, k_in, v_in, go_in, grads,
     places, docs, qbuf, kv, kbuf, scores, dprobs, pair, peaks, masses, weights, lows, highs,
-    logs, deltas, give, take, kept, total, gathered, pieces, dq_part, dq_took,
+    logs, deltas, give, take, total, gathered, pieces, dq_part, dq_took,
     local_sem, send_sem, recv_sem, swap_sem, take_sem,
 ):
     i, h = lax.axis_index("ctx"), lax.axis_index("head")
@@ -61,7 +62,7 @@
     def owner(n):
         g, dz, jj = n // 16, n // 2 % 4 * 2 + n // 8 % 2, n % 2
         where = device(yhs[g], zs[(Z - dz) % Z], x, yjs[jj] * 2 + yp, c)
-        return where, n // 2 * SPAN + yjs[jj] * 32
+        return where, n // 2 * HALF + yjs[jj] * 16
 
     def head_peer(n):
         return device(yh, z, x, yls[n // 2], cs[n % 2])
@@ -110,22 +111,19 @@
 
     for copy in loads:
         copy.wait()
-    half = pl.ds(pl.multiple_of(yp * SPAN, SPAN), SPAN)
-    other = pl.ds(pl.multiple_of((1 - yp) * SPAN, SPAN), SPAN)
-
     pl.semaphore_wait(barrier, 31 + 8 + 7 + 7)
 
     def send_far(a, m):
-        rows = pl.ds(pl.multiple_of(512 + c * 256 + m * SPAN, SPAN), SPAN)
+        rows = pl.ds(pl.multiple_of(256 + c * 128 + m * HALF, HALF), HALF)
         where = device(1 - yh, lax.rem(z + 2 * m + c, Z), x, YL - 1 - yl, c)
-        remote(kv.at[a, other], kbuf.at[a, rows], send_sem.at[0], recv_sem.at[2 * a + 1], where).start()
+        remote(kv.at[a, 1 - yp], kbuf.at[a, :, rows], send_sem.at[0], recv_sem.at[2 * a + 1], where).start()
 
     def send_near(a, m):
-        rows = pl.ds(pl.multiple_of(c * 256 + m * SPAN, SPAN), SPAN)
+        rows = pl.ds(pl.multiple_of(c * 128 + m * HALF, HALF), HALF)
         where = device(yh, lax.rem(z + 2 * m + c, Z), x, yl, c)
 
         def send():
-            remote(kv.at[a, half], kbuf.at[a, rows], send_sem.at[0], recv_sem.at[2 * a], where).start()
+            remote(kv.at[a, yp], kbuf.at[a, :, rows], send_sem.at[0], recv_sem.at[2 * a], where).start()
 
         if m > 0:
             send()
@@ -134,7 +132,7 @@
 
         @pl.when(c == 0)
         def _():
-            pltpu.make_async_copy(kv.at[a, half], kbuf.at[a, pl.ds(0, SPAN)], recv_sem.at[2 * a]).start()
+            pltpu.make_async_copy(kv.at[a, yp], kbuf.at[a, :, pl.ds(0, HALF)], recv_sem.at[2 * a]).start()
 
     def send_query(a, n):
         remote(
@@ -166,46 +164,46 @@
             highs[t // 2, :, (t % 2) * ROWS : (t % 2 + 1) * ROWS] = place
 
     def hand_over(a, g):
-        rows = pl.ds(pl.multiple_of(g * 512 + c * 256, 256), 256)
-        wait_for(kbuf.at[a, rows], recv_sem.at[2 * a + g])
-        remote(kbuf.at[a, rows], kbuf.at[a, rows], swap_sem.at[4], swap_sem.at[2 * a + g], sibling).start()
+        rows = pl.ds(pl.multiple_of(g * 256 + c * 128, 128), 128)
+        block = kbuf.at[a, :, rows]
+        wait_for(block, recv_sem.at[2 * a + g])
+        remote(block, block, swap_sem.at[4], swap_sem.at[2 * a + g], sibling).start()
 
     def handed(a, g):
-        rows = pl.ds(pl.multiple_of(g * 512 + (1 - c) * 256, 256), 256)
-        wait_for(kbuf.at[a, rows], swap_sem.at[2 * a + g])
+        rows = pl.ds(pl.multiple_of(g * 256 + (1 - c) * 128, 128), 128)
+        wait_for(kbuf.at[a, :, rows], swap_sem.at[2 * a + g])
 
     hand_over(0, 0)
     hand_over(0, 1)
     wait_for(qbuf.at[0, pl.ds(ROWS, 7 * ROWS)], recv_sem.at[4])
 
-    row = lax.broadcasted_iota(jnp.int32, (SPAN, LANES), 0)
+    row = lax.broadcasted_iota(jnp.int32, (HALF, LANES), 0)
 
     def product(g, t):
         rows = pl.ds(pl.multiple_of(t * LANES, LANES), LANES)
         low, high = lows[t, 0:1, :], highs[t, 0:1, :]
-        s = lax.dot_general(
-            kbuf[0, g * 512 : g * 512 + 512], qbuf[0, rows], NT, preferred_element_type=jnp.float32
-        )
         peak = None if g == 0 else peaks[t]
-        for n in range(8):
-            behind = zs[(Z - (n % 4 * 2 + n // 4)) % Z]
-            ctx = yhs[g] * (Z * X) + behind * X + x
-            place = places[2 * ctx + yp] * SPAN + row
-            masked = jnp.where(
-                (place >= low) & (place <= high), s[n * SPAN : n * SPAN + SPAN], NEGATIVE
+        for b in range(2):
+            s = lax.dot_general(
+                kbuf[0, b, g * 256 : g * 256 + 256], qbuf[0, rows], NT, preferred_element_type=jnp.float32
             )
-            scores[t, g * 512 + n * SPAN : g * 512 + n * SPAN + SPAN] = masked
-            top = jnp.max(masked.reshape(SPAN // 8, 8, LANES), axis=0)
-            peak = top if peak is None else jnp.maximum(peak, top)
+            for n in range(8):
+                behind = zs[(Z - (n % 4 * 2 + n // 4)) % Z]
+                ctx = yhs[g] * (Z * X) + behind * X + x
+                place = places[2 * ctx + yp] * SPAN + b * HALF + row
+                masked = jnp.where(
+                    (place >= low) & (place <= high), s[n * HALF : n * HALF + HALF], NEGATIVE
+                )
+                first = b * 512 + g * 256 + n * HALF
+                scores[t, first : first + HALF] = masked
+                top = jnp.max(masked.reshape(HALF // 8, 8, LANES), axis=0)
+                peak = top if peak is None else jnp.maximum(peak, top)
         peaks[t] = peak
 
     handed(0, 0)
     loop(0, PARTS, functools.partial(product, 0))
     handed(0, 1)
     loop(0, PARTS, functools.partial(product, 1))
-    hand_over(1, 0)
-    hand_over(1, 1)
-
     def weigh(t):
         peak = jnp.maximum(jnp.max(peaks[t], axis=0, keepdims=True), FLOOR)
 
@@ -228,14 +226,19 @@
         remote(logs.at[0], logs.at[n], send_sem.at[2], recv_sem.at[6], query_peer(n)[0]).start()
 
     each(1, 8, send_logs)
+    hand_over(1, 0)
+    hand_over(1, 1)
 
     def cotangent(g, t):
         rows = pl.ds(pl.multiple_of(t * LANES, LANES), LANES)
-        d = lax.dot_general(
-            kbuf[1, g * 512 : g * 512 + 512], qbuf[1, rows], NT, preferred_element_type=jnp.float32
-        )
-        dprobs[t, g * 512 : g * 512 + 512] = d
-        weighted = jnp.sum((scores[t, g * 512 : g * 512 + 512] * d).reshape(64, 8, LANES), axis=0)
+        weighted = jnp.zeros((8, LANES), jnp.float32)
+        for b in range(2):
+            keys = slice(b * 512 + g * 256, b * 512 + g * 256 + 256)
+            d = lax.dot_general(
+                kbuf[1, b, g * 256 : g * 256 + 256], qbuf[1, rows], NT, preferred_element_type=jnp.float32
+            )
+            dprobs[t, keys] = d
+            weighted += jnp.sum((scores[t, keys] * d).reshape(32, 8, LANES), axis=0)
         if g == 0:
             weights[t] = weighted
         else:
@@ -267,62 +270,68 @@
         _, shares, mass = lse_of(t)
         peaks[t, 1:2] = functools.reduce(jnp.add, [s * deltas[n, t] for n, s in enumerate(shares)]) / mass
 
-    def place_of(r, n):
-        return lax.div(n, 2), pl.ds(pl.multiple_of(r * LANES + lax.rem(n, 2) * CHUNK, CHUNK), CHUNK)
-
-    def value_weights(r):
+    def value_weights(first):
         def step(n):
-            t, rows = place_of(r, n)
+            t, rows = lax.div(n, 2), pl.ds(pl.multiple_of(first + lax.rem(n, 2) * CHUNK, CHUNK), CHUNK)
             pair[1, t, rows] = (scores[t, rows] * peaks[t, 0:1]).astype(jnp.bfloat16)
 
         loop(0, 2 * PARTS, step)
 
-    def key_weights(r):
+    def key_weights(first):
         def step(n):
-            t, rows = place_of(r, n)
+            t, rows = lax.div(n, 2), pl.ds(pl.multiple_of(first + lax.rem(n, 2) * CHUNK, CHUNK), CHUNK)
             probs = scores[t, rows] * peaks[t, 0:1]
             pair[0, t, rows] = (probs * (dprobs[t, rows] - peaks[t, 1:2]) * SCALE).astype(jnp.bfloat16)
 
         loop(0, 2 * PARTS, step)
 
-    def key_side(which, rows):
+    def key_side(which, first):
         acc = jnp.zeros((LANES, WIDTH), jnp.float32)
         for t in range(PARTS):
             acc += jnp.dot(
-                pair[which, t, rows], qbuf[which, t * LANES : t * LANES + LANES],
+                pair[which, t, pl.ds(first, LANES)], qbuf[which, t * LANES : t * LANES + LANES],
                 preferred_element_type=jnp.float32,
             )
         return acc
 
-    def send_piece(n):
+    def send_piece(which, n):
         where, first = owner(n)
-        rows = pl.ds(pl.multiple_of(first, 32), 32)
-        remote(total.at[rows], gathered.at[n - 1], send_sem.at[5], recv_sem.at[9], where).start()
-
-    def settle(r):
-        rows = pl.ds(r * LANES, LANES)
-        wait_for(take.at[rows], take_sem.at[r])
-        total[rows] = (kept[rows] + take[rows].astype(jnp.float32)).astype(jnp.bfloat16)
-        each(max(1, 8 * r), 8 * r + 8, send_piece)
+        rows = pl.ds(pl.multiple_of(first, 16), 16)
+        remote(
+            total.at[which, rows], gathered.at[which, n - 1],
+            send_sem.at[5], recv_sem.at[9 + which], where,
+        ).start()
 
     def one_side(which, weigh_chunk):
-        keeps = c == which
-        for r in (3, 2, 1, 0):
+        for r in (1, 0):
+            first = pl.multiple_of((1 - c) * 512 + r * LANES, LANES)
             rows = pl.ds(r * LANES, LANES)
-            weigh_chunk(r)
-            acc = key_side(which, rows)
-
-            @pl.when(jnp.logical_not(keeps))
-            def _():
-                give[rows] = acc.astype(jnp.bfloat16)
-                remote(give.at[rows], take.at[rows], send_sem.at[3], take_sem.at[r], sibling).start()
-
-            @pl.when(keeps)
-            def _():
-                kept[rows] = acc
-                if r < 3:
-                    settle(r + 1)
-        pl.when(keeps)(lambda: settle(0))
+            weigh_chunk(first)
+            give[which, rows] = key_side(which, first).astype(jnp.bfloat16)
+            remote(
+                give.at[which, rows], take.at[which, rows],
+                send_sem.at[3], take_sem.at[2 * which + r], sibling,
+            ).start()
+        for r in (1, 0):
+            first = pl.multiple_of(c * 512 + r * LANES, LANES)
+            rows = pl.ds(r * LANES, LANES)
+            weigh_chunk(first)
+            acc = key_side(which, first)
+            wait_for(take.at[which, rows], take_sem.at[2 * which + r])
+            total[which, rows] = (acc + take[which, rows].astype(jnp.float32)).astype(jnp.bfloat16)
+            each(max(1, 16 * r), 16 * r + 16, functools.partial(send_piece, which))
+
+    def conclude(which):
+        wait_for(gathered.at[which], recv_sem.at[9 + which])
+        result = total[which, pl.ds(pl.multiple_of(yj * 16, 16), 16)].astype(jnp.float32)
+        for n in range(31):
+            result += gathered[which, n].astype(jnp.float32)
+        pieces[which, 0] = result.astype(jnp.bfloat16)
+        for n in range(1, 8):
+            remote(
+                pieces.at[which, 0], pieces.at[which, n],
+                send_sem.at[6], recv_sem.at[11 + which], head_peer(n),
+            ).start()
 
     wait_for(logs.at[pl.ds(1, 7)], recv_sem.at[6])
     loop(0, PARTS, normalize)
@@ -332,7 +341,8 @@
     one_side(0, key_weights)
 
     def query_side(t):
-        part = lax.dot_general(kbuf[0], pair[0, t], TN, preferred_element_type=jnp.float32)
+        keys = kbuf[0].reshape(TILE, WIDTH)
+        part = lax.dot_general(keys, pair[0, t], TN, preferred_element_type=jnp.float32)
         part = part.astype(dq_part.dtype)
         dq_part[2 * t] = part[:, :ROWS]
         dq_part[2 * t + 1] = part[:, ROWS:]
@@ -345,31 +355,22 @@
 
     each(1, 8, send_dq)
 
+    conclude(1)
     wait_for(dq_took, recv_sem.at[8])
     dq = dq_part[own].astype(jnp.float32)
     for n in range(7):
         dq += dq_took[n].astype(jnp.float32)
     grads[0] = dq.T.astype(jnp.bfloat16)
 
-    first = pl.ds(pl.multiple_of(yj * 32, 32), 32)
-    wait_for(gathered, recv_sem.at[9])
-    result = total[first].astype(jnp.float32)
-    for n in range(31):
-        result += gathered[n].astype(jnp.float32)
-    pieces[0] = result.astype(jnp.bfloat16)
-
-    def send_result(n):
-        remote(pieces.at[0], pieces.at[n], send_sem.at[6], recv_sem.at[10], head_peer(n)).start()
-
-    each(1, 8, send_result)
-    wait_for(pieces.at[pl.ds(1, 7)], recv_sem.at[10])
-    for n in range(YL):
-        fl = lax.rem(yl + YL - n, YL)
-        rows = pl.ds(pl.multiple_of(lax.rem(fl, 2) * SPAN + lax.div(fl, 2) * 32, 32), 32)
-        grads[1, rows] = pieces[2 * n + c]
-        grads[2, rows] = pieces[2 * n + 1 - c]
-
-    pl.when(c == 0)(lambda: wait_for(kbuf.at[0, pl.ds(0, 896)], send_sem.at[0]))
+    conclude(0)
+    for which in (1, 0):
+        wait_for(pieces.at[which, pl.ds(1, 7)], recv_sem.at[11 + which])
+        for n in range(8):
+            fl, fc = yls[(YL - n // 2) % YL], cs[n % 2]
+            first = lax.rem(fl, 2) * SPAN + fc * HALF + lax.div(fl, 2) * 16
+            grads[1 + which, pl.ds(pl.multiple_of(first, 16), 16)] = pieces[which, n]
+
+    pl.when(c == 0)(lambda: wait_for(kbuf.at[0, :, pl.ds(0, 448)], send_sem.at[0]))
     pl.when(c == 1)(lambda: wait_for(kbuf.at[0], send_sem.at[0]))
     wait_for(qbuf.at[:, pl.ds(ROWS, 7 * ROWS)], send_sem.at[1])
     wait_for(kbuf.at[0], swap_sem.at[4])
@@ -378,7 +379,7 @@
     wait_for(give, send_sem.at[3])
     wait_for(dq_took, send_sem.at[4])
     wait_for(gathered, send_sem.at[5])
-    wait_for(pieces.at[pl.ds(1, 7)], send_sem.at[6])
+    wait_for(pieces.at[:, pl.ds(1, 7)], send_sem.at[6])
 
 
 def local(queries, keys, values, grad_out, order, segment):
@@ -393,8 +394,8 @@
             pltpu.SMEM((TOKENS // SPAN,), i32),
             pltpu.VMEM((TOKENS // WIDTH, WIDTH), i32),
             pltpu.VMEM((2, TILE, WIDTH), bf16),
-            pltpu.VMEM((2, ROWS, WIDTH), bf16),
-            pltpu.VMEM((2, TILE, WIDTH), bf16),
+            pltpu.VMEM((2, 2, 2, HALF, WIDTH), bf16),
+            pltpu.VMEM((2, 2, TILE // 2, WIDTH), bf16),
             pltpu.VMEM((PARTS, TILE, LANES), f32),
             pltpu.VMEM((PARTS, TILE, LANES), f32),
             pltpu.VMEM((2, PARTS, TILE, LANES), bf16),
@@ -405,17 +406,16 @@
             pltpu.VMEM((PARTS, 8, LANES), i32),
             pltpu.VMEM((8, PARTS, 1, LANES), f32),
             pltpu.VMEM((8, PARTS, 1, LANES), f32),
-            pltpu.VMEM((TILE, WIDTH), bf16),
-            pltpu.VMEM((TILE, WIDTH), bf16),
-            pltpu.VMEM((TILE, WIDTH), f32),
-            pltpu.VMEM((TILE, WIDTH), bf16),
-            pltpu.VMEM((31, 32, WIDTH), bf16),
-            pltpu.VMEM((8, 32, WIDTH), bf16),
+            pltpu.VMEM((2, TILE // 2, WIDTH), bf16),
+            pltpu.VMEM((2, TILE // 2, WIDTH), bf16),
+            pltpu.VMEM((2, TILE // 2, WIDTH), bf16),
+            pltpu.VMEM((2, 31, 16, WIDTH), bf16),
+            pltpu.VMEM((2, 8, 16, WIDTH), bf16),
             pltpu.VMEM((8, WIDTH, ROWS), bf16),
             pltpu.VMEM((7, WIDTH, ROWS), bf16),
             pltpu.SemaphoreType.DMA((6,)),
             pltpu.SemaphoreType.DMA((8,)),
-            pltpu.SemaphoreType.DMA((11,)),
+            pltpu.SemaphoreType.DMA((13,)),
             pltpu.SemaphoreType.DMA((5,)),
             pltpu.SemaphoreType.DMA((4,)),
         ],
@@ -423,7 +423,14 @@
             collective_id=0, has_side_effects=True, vmem_limit_bytes=55 << 20
         ),
         name="attention_backward",
-    )(order, segment.reshape(-1, WIDTH), queries, keys, values, grad_out)
+    )(
+        order,
+        segment.reshape(-1, WIDTH),
+        queries,
+        keys.reshape(2, 2, HALF, WIDTH),
+        values.reshape(2, 2, HALF, WIDTH),
+        grad_out,
+    )
     return grads[0:1], grads[1], grads[2]
 
 

time: 53.6 us -> 51.5 us (0.961)
  Pallas kernels: 52.1 us -> 50 us
    pallas_call x1, Pallas kernels: 52.1 us -> 50 us  [local(): pl.pallas_call(kernel, out_shape=pltpu.VMEM((3, ROWS, WIDTH), bf16), in_s...]
where the time goes in v4:
time: 51.5 us; the launch traced here: 51.3 us
  Pallas kernels  50 us (97%)
  local copies, waits for them, and re-layouts  0.64 us (1%)
  between operations  0.64 us (1%)
    pallas_call x1, Pallas kernels, local(): pl.pallas_call(kernel, out_shape=pltpu.VMEM((3, ROWS, WIDTH), bf16), in_s...  50 us

profile of v4, /device:TPU:1, one launch (start us, length us, event | category | flops | bytes accessed | tf_op | source)
XLA Modules:
  0.0 51.3 jit_solution(17997285516079663658)
XLA Ops:
  0.6 50.0 %attention_backward.1 = bf16[3,128,128]{2,1,0:T(8,128)(2,1)S(1)} custom-call(s32[128]{0:T(128)} %order_in.1, s32[64,128]{1,0:T(8,128)} %bitcast.7, bf16[1,128,128]{2,1,0:T(8,128)(2,1)} %q_in.1, bf16[2,2,32,128]{3,2,1,0:T(8,128)(2,1)} %bitcast.8, bf16[2,2,32,128]{3,2,1,0:T(8,128)(2,1)} %bitcast.9, bf16[1,128,128]{2,1,0:T(8,128)(2,1)} %go_in.1), custom_call_target="tpu_custom_call" | custom-call | tf_op jit(solution)/shard_map/attention_backward/pallas_call | solution.py:388
  50.6 0.6 %slice_bitcast_fusion = (bf16[128,128]{1,0:T(8,128)(2,1)}, bf16[128,128]{1,0:T(8,128)(2,1)}, bf16[1,128,128]{2,1,0:T(8,128)(2,1)}) fusion(bf16[3,128,128]{2,1,0:T(8,128)(2,1)S(1)} %attention_backward.1), kind=kLoop, calls=%fused_computation | loop fusion | bytes 196608 | tf_op jit(solution)/shard_map/squeeze | solution.py:434

commit v5 on v4

--- a/solution.py
+++ b/solution.py
@@ -34,7 +34,7 @@
 
 def kernel(
     order_in, segment_in, q_in, k_in, v_in, go_in, grads,
-    places, docs, qbuf, kv, kbuf, scores, dprobs, pair, peaks, masses, weights, lows, highs,
+    places, docs, qbuf, kv, kbuf, scores, dprobs, pair, peaks, shares, weights, lows, highs,
     logs, deltas, give, take, total, gathered, pieces, dq_part, dq_took,
     local_sem, send_sem, recv_sem, swap_sem, take_sem,
 ):
@@ -141,9 +141,9 @@
 
     for a in range(2):
         for m in range(4):
+            send_near(a, m)
+        for m in range(4):
             send_far(a, m)
-        for m in range(4):
-            send_near(a, m)
         for n in range(1, 8):
             send_query(a, n)
 
@@ -173,16 +173,12 @@
         rows = pl.ds(pl.multiple_of(g * 256 + (1 - c) * 128, 128), 128)
         wait_for(kbuf.at[a, :, rows], swap_sem.at[2 * a + g])
 
-    hand_over(0, 0)
-    hand_over(0, 1)
-    wait_for(qbuf.at[0, pl.ds(ROWS, 7 * ROWS)], recv_sem.at[4])
-
     row = lax.broadcasted_iota(jnp.int32, (HALF, LANES), 0)
 
     def product(g, t):
         rows = pl.ds(pl.multiple_of(t * LANES, LANES), LANES)
         low, high = lows[t, 0:1, :], highs[t, 0:1, :]
-        peak = None if g == 0 else peaks[t]
+        peak = None
         for b in range(2):
             s = lax.dot_general(
                 kbuf[0, b, g * 256 : g * 256 + 256], qbuf[0, rows], NT, preferred_element_type=jnp.float32
@@ -198,36 +194,35 @@
                 scores[t, first : first + HALF] = masked
                 top = jnp.max(masked.reshape(HALF // 8, 8, LANES), axis=0)
                 peak = top if peak is None else jnp.maximum(peak, top)
-        peaks[t] = peak
-
-    handed(0, 0)
-    loop(0, PARTS, functools.partial(product, 0))
-    handed(0, 1)
-    loop(0, PARTS, functools.partial(product, 1))
-    def weigh(t):
-        peak = jnp.maximum(jnp.max(peaks[t], axis=0, keepdims=True), FLOOR)
-
-        def step(r, carry):
-            rows = pl.ds(pl.multiple_of(r * CHUNK, CHUNK), CHUNK)
+        peaks[g, t] = peak
+
+    def weigh(g, t):
+        peak = jnp.maximum(jnp.max(peaks[g, t], axis=0, keepdims=True), FLOOR)
+
+        def step(n, carry):
+            first = lax.div(n, 2) * 512 + g * 256 + lax.rem(n, 2) * CHUNK
+            rows = pl.ds(pl.multiple_of(first, CHUNK), CHUNK)
             expo = jnp.exp2((scores[t, rows] - peak) * (SCALE * LOG2E))
             scores[t, rows] = expo
             return carry + jnp.sum(expo.reshape(CHUNK // 8, 8, LANES), axis=0)
 
-        mass = lax.fori_loop(0, TILE // CHUNK, step, jnp.zeros((8, LANES), jnp.float32))
-        mass = jnp.maximum(jnp.sum(mass, axis=0, keepdims=True), 1e-30)
+        mass = lax.fori_loop(0, 4, step, jnp.zeros((8, LANES), jnp.float32))
+        mass = jnp.sum(mass, axis=0, keepdims=True)
         peak = peak * (SCALE * LOG2E)
-        peaks[t, 0:1] = peak
-        masses[t] = mass
-        logs[0, t] = peak + jnp.log2(mass)
-
-    loop(0, PARTS, weigh)
+        peaks[g, t, 0:1] = peak
+        if g == 0:
+            shares[0, t] = mass
+            return
+        peak_near = peaks[0, t, 0:1]
+        top = jnp.maximum(peak_near, peak)
+        near, far = jnp.exp2(peak_near - top), jnp.exp2(peak - top)
+        mass = jnp.maximum(near * shares[0, t] + far * mass, 1e-30)
+        shares[0, t] = near / mass
+        shares[1, t] = far / mass
+        logs[0, t] = top + jnp.log2(mass)
 
     def send_logs(n):
         remote(logs.at[0], logs.at[n], send_sem.at[2], recv_sem.at[6], query_peer(n)[0]).start()
-
-    each(1, 8, send_logs)
-    hand_over(1, 0)
-    hand_over(1, 1)
 
     def cotangent(g, t):
         rows = pl.ds(pl.multiple_of(t * LANES, LANES), LANES)
@@ -239,12 +234,24 @@
             )
             dprobs[t, keys] = d
             weighted += jnp.sum((scores[t, keys] * d).reshape(32, 8, LANES), axis=0)
+        weighted = jnp.sum(weighted, axis=0, keepdims=True)
         if g == 0:
             weights[t] = weighted
         else:
-            weighted = jnp.sum(weights[t] + weighted, axis=0, keepdims=True)
-            deltas[0, t] = weighted / masses[t]
-
+            deltas[0, t] = weights[t] * shares[0, t] + weighted * shares[1, t]
+
+    hand_over(0, 0)
+    wait_for(qbuf.at[0, pl.ds(ROWS, 7 * ROWS)], recv_sem.at[4])
+    handed(0, 0)
+    loop(0, PARTS, functools.partial(product, 0))
+    loop(0, PARTS, functools.partial(weigh, 0))
+    hand_over(0, 1)
+    hand_over(1, 0)
+    handed(0, 1)
+    loop(0, PARTS, functools.partial(product, 1))
+    loop(0, PARTS, functools.partial(weigh, 1))
+    each(1, 8, send_logs)
+    hand_over(1, 1)
     wait_for(qbuf.at[1, pl.ds(ROWS, 7 * ROWS)], recv_sem.at[5])
     handed(1, 0)
     loop(0, PARTS, functools.partial(cotangent, 0))
@@ -259,29 +266,30 @@
     def lse_of(t):
         every = [logs[n, t] for n in range(8)]
         top = functools.reduce(jnp.maximum, every)
-        shares = [jnp.exp2(e - top) for e in every]
-        return top, shares, functools.reduce(jnp.add, shares)
+        parts = [jnp.exp2(e - top) for e in every]
+        return top, parts, functools.reduce(jnp.add, parts)
 
     def normalize(t):
         top, _, mass = lse_of(t)
-        peaks[t, 0:1] = jnp.exp2(peaks[t, 0:1] - top) / mass
+        for g in range(2):
+            peaks[g, t, 0:1] = jnp.exp2(peaks[g, t, 0:1] - top) / mass
 
     def center(t):
-        _, shares, mass = lse_of(t)
-        peaks[t, 1:2] = functools.reduce(jnp.add, [s * deltas[n, t] for n, s in enumerate(shares)]) / mass
-
-    def value_weights(first):
+        _, parts, mass = lse_of(t)
+        peaks[0, t, 1:2] = functools.reduce(jnp.add, [s * deltas[n, t] for n, s in enumerate(parts)]) / mass
+
+    def value_weights(first, g):
         def step(n):
             t, rows = lax.div(n, 2), pl.ds(pl.multiple_of(first + lax.rem(n, 2) * CHUNK, CHUNK), CHUNK)
-            pair[1, t, rows] = (scores[t, rows] * peaks[t, 0:1]).astype(jnp.bfloat16)
+            pair[1, t, rows] = (scores[t, rows] * peaks[g, t, 0:1]).astype(jnp.bfloat16)
 
         loop(0, 2 * PARTS, step)
 
-    def key_weights(first):
+    def key_weights(first, g):
         def step(n):
             t, rows = lax.div(n, 2), pl.ds(pl.multiple_of(first + lax.rem(n, 2) * CHUNK, CHUNK), CHUNK)
-            probs = scores[t, rows] * peaks[t, 0:1]
-            pair[0, t, rows] = (probs * (dprobs[t, rows] - peaks[t, 1:2]) * SCALE).astype(jnp.bfloat16)
+            probs = scores[t, rows] * peaks[g, t, 0:1]
+            pair[0, t, rows] = (probs * (dprobs[t, rows] - peaks[0, t, 1:2]) * SCALE).astype(jnp.bfloat16)
 
         loop(0, 2 * PARTS, step)
 
@@ -306,7 +314,7 @@
         for r in (1, 0):
             first = pl.multiple_of((1 - c) * 512 + r * LANES, LANES)
             rows = pl.ds(r * LANES, LANES)
-            weigh_chunk(first)
+            weigh_chunk(first, r)
             give[which, rows] = key_side(which, first).astype(jnp.bfloat16)
             remote(
                 give.at[which, rows], take.at[which, rows],
@@ -315,7 +323,7 @@
         for r in (1, 0):
             first = pl.multiple_of(c * 512 + r * LANES, LANES)
             rows = pl.ds(r * LANES, LANES)
-            weigh_chunk(first)
+            weigh_chunk(first, r)
             acc = key_side(which, first)
             wait_for(take.at[which, rows], take_sem.at[2 * which + r])
             total[which, rows] = (acc + take[which, rows].astype(jnp.float32)).astype(jnp.bfloat16)
@@ -399,9 +407,9 @@
             pltpu.VMEM((PARTS, TILE, LANES), f32),
             pltpu.VMEM((PARTS, TILE, LANES), f32),
             pltpu.VMEM((2, PARTS, TILE, LANES), bf16),
-            pltpu.VMEM((PARTS, 8, LANES), f32),
+            pltpu.VMEM((2, PARTS, 8, LANES), f32),
+            pltpu.VMEM((2, PARTS, 1, LANES), f32),
             pltpu.VMEM((PARTS, 1, LANES), f32),
-            pltpu.VMEM((PARTS, 8, LANES), f32),
             pltpu.VMEM((PARTS, 8, LANES), i32),
             pltpu.VMEM((PARTS, 8, LANES), i32),
             pltpu.VMEM((8, PARTS, 1, LANES), f32),

time: 51.5 us -> 52.1 us (1.012)
  Pallas kernels: 50 us -> 50.6 us
    pallas_call x1, Pallas kernels: 50 us -> 50.6 us  [local(): pl.pallas_call(kernel, out_shape=pltpu.VMEM((3, ROWS, WIDTH), bf16), in_s...]
where the time goes in v5:
time: 52.1 us; the launch traced here: 51.9 us
  Pallas kernels  50.6 us (97%)
  local copies, waits for them, and re-layouts  0.64 us (1%)
  between operations  0.64 us (1%)
    pallas_call x1, Pallas kernels, local(): pl.pallas_call(kernel, out_shape=pltpu.VMEM((3, ROWS, WIDTH), bf16), in_s...  50.6 us

profile of v5, /device:TPU:1, one launch (start us, length us, event | category | flops | bytes accessed | tf_op | source)
XLA Modules:
  0.0 51.9 jit_solution(2131256881441259079)
XLA Ops:
  0.6 50.6 %attention_backward.1 = bf16[3,128,128]{2,1,0:T(8,128)(2,1)S(1)} custom-call(s32[128]{0:T(128)} %order_in.1, s32[64,128]{1,0:T(8,128)} %bitcast.7, bf16[1,128,128]{2,1,0:T(8,128)(2,1)} %q_in.1, bf16[2,2,32,128]{3,2,1,0:T(8,128)(2,1)} %bitcast.8, bf16[2,2,32,128]{3,2,1,0:T(8,128)(2,1)} %bitcast.9, bf16[1,128,128]{2,1,0:T(8,128)(2,1)} %go_in.1), custom_call_target="tpu_custom_call" | custom-call | tf_op jit(solution)/shard_map/attention_backward/pallas_call | solution.py:396
  51.3 0.6 %slice_bitcast_fusion = (bf16[128,128]{1,0:T(8,128)(2,1)}, bf16[128,128]{1,0:T(8,128)(2,1)}, bf16[1,128,128]{2,1,0:T(8,128)(2,1)}) fusion(bf16[3,128,128]{2,1,0:T(8,128)(2,1)S(1)} %attention_backward.1), kind=kLoop, calls=%fused_computation | loop fusion | bytes 196608 | tf_op jit(solution)/shard_map/squeeze | solution.py:442

commit v6 on v5

--- a/solution.py
+++ b/solution.py
@@ -34,7 +34,7 @@
 
 def kernel(
     order_in, segment_in, q_in, k_in, v_in, go_in, grads,
-    places, docs, qbuf, kv, kbuf, scores, dprobs, pair, peaks, shares, weights, lows, highs,
+    places, docs, qbuf, kv, mirrored, kbuf, scores, dprobs, pair, peaks, shares, weights, lows, highs,
     logs, deltas, give, take, total, gathered, pieces, dq_part, dq_took,
     local_sem, send_sem, recv_sem, swap_sem, take_sem,
 ):
@@ -56,8 +56,11 @@
     def near_peer(n):
         return device(yh, zs[n], x, yl, c)
 
-    def far_peer(n):
-        return device(1 - yh, zs[n], x, YL - 1 - yl, c)
+    mirror = device(1 - yh, z, x, YL - 1 - yl, c)
+
+    def line_peer(n):
+        q = lax.rem(yh * 2 + yj + n // 2, 4)
+        return device(lax.div(q, 2), z, x, lax.rem(q, 2) * 2 + yp, cs[n % 2])
 
     def owner(n):
         g, dz, jj = n // 16, n // 2 % 4 * 2 + n // 8 % 2, n % 2
@@ -104,26 +107,25 @@
     def greet(where):
         pl.semaphore_signal(barrier, inc=1, device_id=where, device_id_type=MESH)
 
-    each(1, 32, lambda n: greet(owner(n)[0]))
-    each(0, 8, lambda n: greet(far_peer(n)))
+    each(2, 8, lambda n: greet(line_peer(n)))
+    each(1, 8, lambda n: greet(near_peer(n)))
+    greet(mirror)
     each(1, 8, lambda n: greet(query_peer(n)[0]))
     each(1, 8, lambda n: greet(head_peer(n)))
 
     for copy in loads:
         copy.wait()
-    pl.semaphore_wait(barrier, 31 + 8 + 7 + 7)
-
-    def send_far(a, m):
-        rows = pl.ds(pl.multiple_of(256 + c * 128 + m * HALF, HALF), HALF)
-        where = device(1 - yh, lax.rem(z + 2 * m + c, Z), x, YL - 1 - yl, c)
-        remote(kv.at[a, 1 - yp], kbuf.at[a, :, rows], send_sem.at[0], recv_sem.at[2 * a + 1], where).start()
-
-    def send_near(a, m):
-        rows = pl.ds(pl.multiple_of(c * 128 + m * HALF, HALF), HALF)
+    pl.semaphore_wait(barrier, 6 + 7 + 1 + 7 + 7)
+
+    def send_mirror(a):
+        remote(kv.at[a, 1 - yp], mirrored.at[a], send_sem.at[8], recv_sem.at[13 + a], mirror).start()
+
+    def send_along(block, a, g, m):
+        rows = pl.ds(pl.multiple_of(g * 256 + c * 128 + m * HALF, HALF), HALF)
         where = device(yh, lax.rem(z + 2 * m + c, Z), x, yl, c)
 
         def send():
-            remote(kv.at[a, yp], kbuf.at[a, :, rows], send_sem.at[0], recv_sem.at[2 * a], where).start()
+            remote(block, kbuf.at[a, :, rows], send_sem.at[0], recv_sem.at[2 * a + g], where).start()
 
         if m > 0:
             send()
@@ -132,18 +134,19 @@
 
         @pl.when(c == 0)
         def _():
-            pltpu.make_async_copy(kv.at[a, yp], kbuf.at[a, :, pl.ds(0, HALF)], recv_sem.at[2 * a]).start()
+            slot = kbuf.at[a, :, pl.ds(g * 256, HALF)]
+            pltpu.make_async_copy(block, slot, recv_sem.at[2 * a + g]).start()
 
     def send_query(a, n):
         remote(
             qbuf.at[a, mine], qbuf.at[a, mine], send_sem.at[1], recv_sem.at[4 + a], query_peer(n)[0]
         ).start()
 
+    send_mirror(0)
+    send_mirror(1)
     for a in range(2):
         for m in range(4):
-            send_near(a, m)
-        for m in range(4):
-            send_far(a, m)
+            send_along(kv.at[a, yp], a, 0, m)
         for n in range(1, 8):
             send_query(a, n)
 
@@ -240,18 +243,22 @@
         else:
             deltas[0, t] = weights[t] * shares[0, t] + weighted * shares[1, t]
 
+    for a in range(2):
+        wait_for(mirrored.at[a], recv_sem.at[13 + a])
+        for m in range(4):
+            send_along(mirrored.at[a], a, 1, m)
     hand_over(0, 0)
     wait_for(qbuf.at[0, pl.ds(ROWS, 7 * ROWS)], recv_sem.at[4])
     handed(0, 0)
     loop(0, PARTS, functools.partial(product, 0))
+    hand_over(1, 0)
     loop(0, PARTS, functools.partial(weigh, 0))
     hand_over(0, 1)
-    hand_over(1, 0)
+    hand_over(1, 1)
     handed(0, 1)
     loop(0, PARTS, functools.partial(product, 1))
     loop(0, PARTS, functools.partial(weigh, 1))
     each(1, 8, send_logs)
-    hand_over(1, 1)
     wait_for(qbuf.at[1, pl.ds(ROWS, 7 * ROWS)], recv_sem.at[5])
     handed(1, 0)
     loop(0, PARTS, functools.partial(cotangent, 0))
@@ -378,7 +385,8 @@
             first = lax.rem(fl, 2) * SPAN + fc * HALF + lax.div(fl, 2) * 16
             grads[1 + which, pl.ds(pl.multiple_of(first, 16), 16)] = pieces[which, n]
 
-    pl.when(c == 0)(lambda: wait_for(kbuf.at[0, :, pl.ds(0, 448)], send_sem.at[0]))
+    wait_for(mirrored, send_sem.at[8])
+    pl.when(c == 0)(lambda: wait_for(kbuf.at[0, :, pl.ds(0, 384)], send_sem.at[0]))
     pl.when(c == 1)(lambda: wait_for(kbuf.at[0], send_sem.at[0]))
     wait_for(qbuf.at[:, pl.ds(ROWS, 7 * ROWS)], send_sem.at[1])
     wait_for(kbuf.at[0], swap_sem.at[4])
@@ -403,6 +411,7 @@
             pltpu.VMEM((TOKENS // WIDTH, WIDTH), i32),
             pltpu.VMEM((2, TILE, WIDTH), bf16),
             pltpu.VMEM((2, 2, 2, HALF, WIDTH), bf16),
+            pltpu.VMEM((2, 2, HALF, WIDTH), bf16),
             pltpu.VMEM((2, 2, TILE // 2, WIDTH), bf16),
             pltpu.VMEM((PARTS, TILE, LANES), f32),
             pltpu.VMEM((PARTS, TILE, LANES), f32),
@@ -422,8 +431,8 @@
             pltpu.VMEM((8, WIDTH, ROWS), bf16),
             pltpu.VMEM((7, WIDTH, ROWS), bf16),
             pltpu.SemaphoreType.DMA((6,)),
-            pltpu.SemaphoreType.DMA((8,)),
-            pltpu.SemaphoreType.DMA((13,)),
+            pltpu.SemaphoreType.DMA((9,)),
+            pltpu.SemaphoreType.DMA((15,)),
             pltpu.SemaphoreType.DMA((5,)),
             pltpu.SemaphoreType.DMA((4,)),
         ],

time: 52.1 us -> 48.4 us (0.929)
  Pallas kernels: 50.6 us -> 46.9 us
    pallas_call x1, Pallas kernels: 50.6 us -> 46.9 us  [local(): pl.pallas_call(kernel, out_shape=pltpu.VMEM((3, ROWS, WIDTH), bf16), in_s...]
where the time goes in v6:
time: 48.4 us; the launch traced here: 48.2 us
  Pallas kernels  46.9 us (97%)
  local copies, waits for them, and re-layouts  0.64 us (1%)
  between operations  0.64 us (1%)
    pallas_call x1, Pallas kernels, local(): pl.pallas_call(kernel, out_shape=pltpu.VMEM((3, ROWS, WIDTH), bf16), in_s...  46.9 us

profile of v6, /device:TPU:1, one launch (start us, length us, event | category | flops | bytes accessed | tf_op | source)
XLA Modules:
  0.0 48.2 jit_solution(17200926668129920582)
XLA Ops:
  0.6 46.9 %attention_backward.1 = bf16[3,128,128]{2,1,0:T(8,128)(2,1)S(1)} custom-call(s32[128]{0:T(128)} %order_in.1, s32[64,128]{1,0:T(8,128)} %bitcast.7, bf16[1,128,128]{2,1,0:T(8,128)(2,1)} %q_in.1, bf16[2,2,32,128]{3,2,1,0:T(8,128)(2,1)} %bitcast.8, bf16[2,2,32,128]{3,2,1,0:T(8,128)(2,1)} %bitcast.9, bf16[1,128,128]{2,1,0:T(8,128)(2,1)} %go_in.1), custom_call_target="tpu_custom_call" | custom-call | tf_op jit(solution)/shard_map/attention_backward/pallas_call | solution.py:404
  47.5 0.6 %slice_bitcast_fusion = (bf16[128,128]{1,0:T(8,128)(2,1)}, bf16[128,128]{1,0:T(8,128)(2,1)}, bf16[1,128,128]{2,1,0:T(8,128)(2,1)}) fusion(bf16[3,128,128]{2,1,0:T(8,128)(2,1)S(1)} %attention_backward.1), kind=kLoop, calls=%fused_computation | loop fusion | bytes 196608 | tf_op jit(solution)/shard_map/squeeze | solution.py:451
